TPU v7x, 512 devices: a whole 4x4x16 slice. The times are simulated.
512 devices in a mesh: pulse: 128 (over z, y, x_lo), rng: 4 (over x_hi, core).
Axes of the slice: x: 4 (x_hi: 2, x_lo: 2; x = x_hi * 2 + x_lo), y: 4, z: 16, core: 2. Of those that a mesh axis runs over, the one named last changes fastest.
Arguments:
- raw: float32 [2, 2048, 24576], P(None, 'pulse', 'rng'), may hold values from -6 to 6
- range_filter: float32 [2, 24576], replicated, may hold values from -4 to 4
- azimuth_filter: float32 [2, 24576, 2048], P(None, ('pulse', 'rng')), may hold values from -4 to 4
- shifts: int32 [2048], replicated, may hold values from 0 to 16, as said below
- frac_index: int32 [2048], replicated, may hold values from 0 to 15
- kernel_table: float32 [16, 8], replicated, may hold values from 0.05 to 1
Outputs:
- image: float32 [2, 24576, 2048], P(None, ('pulse', 'rng'))
Inputs may be any that keep to these rules, and one draw needn't show every extreme that they name: shifts[0] is 0 and shifts[1024] is 16.
All inputs are finite; a program needn't handle non-finite values.
Results may differ from a plain program's by a relative error of at most 0.000071.
Values sent between devices are 32-bit elements; how exact they have to be, the bound alone decides.
A program may use at most 64 MiB of HBM per device.

v0:
```python
import functools
import math

import jax
import jax.numpy as jnp
import ml_dtypes
import numpy as np
from jax import lax
from jax.experimental import pallas as pl
from jax.experimental.pallas import tpu as pltpu
from jax.sharding import PartitionSpec as P

MESH = pl.DeviceIdType.MESH
F32 = jnp.float32
BF16 = jnp.bfloat16

PULSES = 2048
SAMPLES = 24576
ROWS = 192
LANES = 128
PLANES = 16
PEERS = 32
LANE_PULSES = 4
BINS = 48
SEGMENT = 1536
SEG_ROWS = 12
BLOCK = 2 * SEG_ROWS * LANE_PULSES
BELOW = 8
ABOVE = 24
WINDOW = BELOW + BINS + ABOVE
TAPS = 8


def turn(product, period, sign):
    angle = sign * 2.0 * math.pi * (product % period) / period
    return np.cos(angle), np.sin(angle)


def halves(table):
    high = table.astype(ml_dtypes.bfloat16)
    low = (table - high.astype(np.float64)).astype(ml_dtypes.bfloat16)
    return high, low


def left_factor(table):
    high, low = halves(table)
    return np.concatenate([high, high, low], axis=1)


def right_factor(table):
    high, low = halves(table)
    return np.concatenate([high, high, low], axis=-2)


def lane_bins():
    lanes = np.arange(LANES)
    return 8 * (lanes % 16) + lanes // 16


def table_first():
    ids = np.arange(ROWS)
    re, im = turn(np.outer(ids, ids), ROWS, -1)
    return left_factor(np.block([[re, -im], [im, re]]))


def table_last():
    ids = np.arange(ROWS)
    re, im = turn(np.outer(ids, ids), ROWS, 1)
    re, im = re / SAMPLES, im / SAMPLES
    real_rows = np.concatenate([re, -im], axis=1).reshape(PLANES, 1, SEG_ROWS, 2 * ROWS)
    imag_rows = np.concatenate([im, re], axis=1).reshape(PLANES, 1, SEG_ROWS, 2 * ROWS)
    return left_factor(np.concatenate([real_rows, imag_rows], axis=1).reshape(2 * ROWS, 2 * ROWS))


def filter_order():
    lanes = np.arange(LANES)
    return 2 * (lanes % 64) + lanes // 64


def table_columns(rows, cols, sign, scale=1.0):
    re, im = turn(np.outer(rows, cols), LANES, sign)
    return np.block([[re, im], [-im, re]]) * scale


def table_twist():
    re, im = turn(np.outer(np.arange(ROWS), np.arange(LANES)), SAMPLES, -1)
    return np.stack([re, im]).astype(np.float32)


def table_planes():
    place = np.arange(PEERS)[:, None, None, None]
    r = np.arange(LANE_PULSES)[None, :, None, None]
    z = np.arange(PLANES)[None, None, :, None]
    k1 = np.arange(16)[None, None, None, :]
    re, im = turn((128 * z + 4 * place + r) * k1, PULSES, -1)
    full = np.zeros((PEERS, 2, LANE_PULSES, PLANES, 16, 2, LANE_PULSES))
    for q in range(LANE_PULSES):
        full[:, 0, q, :, :, 0, q] = re[:, q]
        full[:, 1, q, :, :, 0, q] = -im[:, q]
        full[:, 0, q, :, :, 1, q] = im[:, q]
        full[:, 1, q, :, :, 1, q] = re[:, q]
    return right_factor(full.reshape(PEERS, 128, 128))


def table_azimuth():
    place = np.arange(PEERS)[:, None, None]
    r = np.arange(LANE_PULSES)[None, :, None]
    re, im = turn((4 * place + r) * lane_bins()[None, None, :], LANES, -1)
    full = np.zeros((PEERS, 2, LANE_PULSES, 2, LANES))
    full[:, 0, :, 0] = re
    full[:, 1, :, 0] = -im
    full[:, 0, :, 1] = im
    full[:, 1, :, 1] = re
    return right_factor(full.reshape(2 * LANES, 2 * LANES))


def table_back():
    return right_factor(table_columns(lane_bins(), np.arange(LANES), 1, 1.0 / PULSES))


def table_back_twist():
    re, im = turn(np.outer(np.arange(16), np.arange(LANES)), PULSES, 1)
    return np.stack([re, im]).astype(np.float32)


def split(values):
    high = values.astype(BF16)
    low = (values - high.astype(F32)).astype(BF16)
    return high, low


def times_left(table, values):
    high, low = split(values)
    return jnp.dot(table, jnp.concatenate([high, low, high], axis=0), preferred_element_type=F32)


def times_right(values, table):
    high, low = split(values)
    return jnp.dot(jnp.concatenate([high, low, high], axis=1), table, preferred_element_type=F32)


def cmul(a_re, a_im, b_re, b_im):
    return a_re * b_re - a_im * b_im, a_re * b_im + a_im * b_re


def fft_list(values, sign):
    count = len(values)
    if count == 1:
        return values
    even = fft_list(values[0::2], sign)
    odd = fft_list(values[1::2], sign)
    low, high = [], []
    for k in range(count // 2):
        re, im = odd[k]
        if 4 * k == count:
            re, im = (-im, re) if sign > 0 else (im, -re)
        elif k:
            w_re = math.cos(2.0 * math.pi * k / count)
            w_im = sign * math.sin(2.0 * math.pi * k / count)
            re, im = re * w_re - im * w_im, re * w_im + im * w_re
        low.append((even[k][0] + re, even[k][1] + im))
        high.append((even[k][0] - re, even[k][1] - im))
    return low + high


def swap_blocks(arrays, width):
    arrays = list(arrays)
    lane = lax.broadcasted_iota(jnp.int32, arrays[0].shape, 1)
    for bit in (1, 2, 4, 8):
        keep = (lane // width) & bit == 0
        for a in range(16):
            if a & bit:
                continue
            first, second = arrays[a], arrays[a + bit]
            arrays[a] = jnp.where(keep, first, pltpu.roll(second, bit * width, 1))
            arrays[a + bit] = jnp.where(keep, pltpu.roll(first, LANES - bit * width, 1), second)
    return arrays


def compress_kernel(x_ref, filt_ref, first_ref, last_ref, twist_ref, fwd_ref, back_ref, y_ref):
    twist_re, twist_im = twist_ref[0], twist_ref[1]
    filt = []
    for c in range(2):
        cols = [filt_ref[pl.ds(2 * u + c, 64, stride=6), :].T for u in range(3)]
        tall = jnp.concatenate(cols, axis=0)
        filt.append(jnp.concatenate([tall[:ROWS], tall[ROWS:]], axis=1))
    for r in range(LANE_PULSES):
        x = jnp.concatenate(
            [x_ref[pl.ds(c * 768 + r, ROWS, stride=LANE_PULSES), :] for c in range(2)], axis=0
        )
        v = times_left(first_ref[...], x)
        re, im = cmul(v[:ROWS], v[ROWS:], twist_re, twist_im)
        s = times_right(jnp.concatenate([re, im], axis=1), fwd_ref[...])
        re, im = cmul(s[:, :LANES], s[:, LANES:], filt[0], filt[1])
        s = times_right(jnp.concatenate([re, im], axis=1), back_ref[...])
        re, im = cmul(s[:, :LANES], s[:, LANES:], twist_re, -twist_im)
        out = times_left(last_ref[...], jnp.concatenate([re, im], axis=0))
        for z in range(PLANES):
            start = BLOCK * z + 2 * SEG_ROWS * r
            y_ref[start : start + 2 * SEG_ROWS] = out[2 * SEG_ROWS * z : 2 * SEG_ROWS * (z + 1)]


def plane_kernel(z_ref, table_hbm, t_ref, table_ref, sem):
    place = 4 * lax.rem(lax.axis_index("pulse"), 8) + lax.axis_index("rng")
    copy = pltpu.make_async_copy(table_hbm.at[place], table_ref, sem)
    copy.start()
    copy.wait()

    def step(row, _):
        parts = []
        for c in range(2):
            for r in range(LANE_PULSES):
                start = 2 * SEG_ROWS * r + SEG_ROWS * c + row
                parts.append(z_ref[pl.ds(start, PLANES, stride=BLOCK), :])
        t_ref[pl.ds(pl.multiple_of(row * LANES, LANES), LANES), :] = times_right(
            jnp.concatenate(parts, axis=0).T, table_ref[...]
        )
        return 0

    lax.fori_loop(0, SEG_ROWS, step, 0)


def azimuth_kernel(
    g_ref, azf_ref, shift_ref, frac_ref, ktab_ref, fwd_ref, back_ref, twist_ref, out_ref,
    h_ref, d_ref, e_ref, a_ref, f_ref, w_ref,
):
    def turn_group(step, _):
        rows = pl.ds(pl.multiple_of(8 * step, 8), 8)
        for half in range(2):
            got = swap_blocks([g_ref[16 * half + i, rows, :] for i in range(16)], 8)
            for k1 in range(16):
                h_ref[k1, rows, LANES * half : LANES * (half + 1)] = got[k1]
        return 0

    lax.fori_loop(0, WINDOW // 8, turn_group, 0)

    def turn_filter(step, _):
        rows = pl.ds(pl.multiple_of(8 * step, 8), 8)
        for c in range(2):
            got = swap_blocks(
                [azf_ref[c, rows, LANES * t : LANES * (t + 1)] for t in range(16)], 1
            )
            for k1 in range(16):
                a_ref[c, k1, rows, :] = got[k1]
        return 0

    lax.fori_loop(0, BINS // 8, turn_filter, 0)

    frac = frac_ref[...]
    for tap in range(TAPS):
        weight = jnp.zeros(frac.shape, F32)
        for row in range(16):
            weight = jnp.where(frac == row, ktab_ref[row, tap], weight)
        w_ref[tap] = weight

    def per_bin(k1, _):
        d = times_right(h_ref[k1], fwd_ref[...])
        shift = shift_ref[pl.ds(k1, 1), :]
        weights = [w_ref[tap, pl.ds(k1, 1), :] for tap in range(TAPS)]
        moved = []
        for c in range(2):
            x = d[:, LANES * c : LANES * (c + 1)]
            near = jnp.where((shift & 16) != 0, x[16:80], x[0:64])
            x = jnp.concatenate([near, x[64:80]], axis=0)
            d_ref[c, 0:72] = jnp.where((shift & 8) != 0, x[8:80], x[0:72])
            e_ref[c, 0:64] = jnp.where((shift & 4) != 0, d_ref[c, 4:68], d_ref[c, 0:64])
            d_ref[c, 0:62] = jnp.where((shift & 2) != 0, e_ref[c, 2:64], e_ref[c, 0:62])
            e_ref[c, 0:61] = jnp.where((shift & 1) != 0, d_ref[c, 1:62], d_ref[c, 0:61])
            total = weights[0] * e_ref[c, 5 : 5 + BINS]
            for tap in range(1, TAPS):
                total = total + weights[tap] * e_ref[c, 5 + tap : 5 + tap + BINS]
            moved.append(total)
        re, im = cmul(moved[0], moved[1], a_ref[0, k1], a_ref[1, k1])
        s = times_right(jnp.concatenate([re, im], axis=1), back_ref[...])
        re, im = cmul(
            s[:, :LANES], s[:, LANES:], twist_ref[0, pl.ds(k1, 1), :], twist_ref[1, pl.ds(k1, 1), :]
        )
        f_ref[0, k1] = re
        f_ref[1, k1] = im
        return 0

    lax.fori_loop(0, 16, per_bin, 0)

    def finish(step, _):
        rows = pl.ds(pl.multiple_of(8 * step, 8), 8)
        got = fft_list([(f_ref[0, k1, rows, :], f_ref[1, k1, rows, :]) for k1 in range(16)], 1)
        for tile in range(16):
            out_ref[0, rows, LANES * tile : LANES * (tile + 1)] = got[tile][0]
            out_ref[1, rows, LANES * tile : LANES * (tile + 1)] = got[tile][1]
        return 0

    lax.fori_loop(0, BINS // 8, finish, 0)


def range_exchange_kernel(raw_ref, x_ref, send_sem, recv_sem, own_sem):
    me = lax.axis_index("rng")
    barrier = pltpu.get_barrier_semaphore()
    for off in range(1, 4):
        pl.semaphore_signal(
            barrier, inc=1, device_id={"rng": lax.rem(me + off, 4)}, device_id_type=MESH
        )
    pl.semaphore_wait(barrier, 3)
    copies = []
    for off in range(1, 4):
        to = lax.rem(me + off, 4)
        copy = pltpu.make_async_remote_copy(
            src_ref=raw_ref.at[:, lax.div(to, 2), :, lax.rem(to, 2)],
            dst_ref=x_ref.at[:, pl.ds(48 * me, 48)],
            send_sem=send_sem.at[off],
            recv_sem=recv_sem.at[off],
            device_id={"rng": to},
            device_id_type=MESH,
        )
        copy.start()
        copies.append(copy)
    own = pltpu.make_async_copy(
        raw_ref.at[:, lax.div(me, 2), :, lax.rem(me, 2)], x_ref.at[:, pl.ds(48 * me, 48)], own_sem
    )
    own.start()
    own.wait()
    for copy in copies:
        copy.wait()


def plane_peers(z, off, place):
    to = lax.rem(place + off, PEERS)
    return to, (8 * z + lax.div(to, 4), lax.rem(to, 4))


def z_exchange_kernel(y_ref, z_ref, send_sem, recv_sem, own_sem):
    pulse = lax.axis_index("pulse")
    me = lax.div(pulse, 8)
    rest = lax.rem(pulse, 8)
    barrier = pltpu.get_barrier_semaphore()
    for off in range(1, PLANES):
        to = lax.rem(me + off, PLANES)
        pl.semaphore_signal(barrier, inc=1, device_id={"pulse": 8 * to + rest}, device_id_type=MESH)
    pl.semaphore_wait(barrier, PLANES - 1)
    copies = []
    for near in range(1, 9):
        for off in sorted({near, PLANES - near}):
            to = lax.rem(me + off, PLANES)
            copy = pltpu.make_async_remote_copy(
                src_ref=y_ref.at[pl.ds(pl.multiple_of(BLOCK * to, 8), BLOCK)],
                dst_ref=z_ref.at[pl.ds(pl.multiple_of(BLOCK * me, 8), BLOCK)],
                send_sem=send_sem.at[off],
                recv_sem=recv_sem.at[off],
                device_id={"pulse": 8 * to + rest},
                device_id_type=MESH,
            )
            copy.start()
            copies.append(copy)
    mine = pl.ds(pl.multiple_of(BLOCK * me, 8), BLOCK)
    own = pltpu.make_async_copy(y_ref.at[mine], z_ref.at[mine], own_sem)
    own.start()
    own.wait()
    for copy in copies:
        copy.wait()


def plane_exchange_kernel(t_ref, zero_ref, g_ref, send_sem, recv_sem, halo_send, halo_recv, own_sem, zero_sem):
    pulse = lax.axis_index("pulse")
    z = lax.div(pulse, 8)
    place = 4 * lax.rem(pulse, 8) + lax.axis_index("rng")
    first = place == 0
    last = place == PEERS - 1
    barrier = pltpu.get_barrier_semaphore()

    def signal(device):
        pl.semaphore_signal(barrier, inc=1, device_id=device, device_id_type=MESH)

    def greet(off, _):
        signal(plane_peers(z, off, place)[1])
        return 0

    lax.fori_loop(1, PEERS, greet, 0)

    def greet_halo(other):
        def body(off, _):
            signal(plane_peers(other, off, place)[1])
            return 0

        lax.fori_loop(0, PEERS, body, 0)

    has_below = z > 0
    has_above = z < PLANES - 1
    takes_below = jnp.logical_and(first, has_below)
    takes_above = jnp.logical_and(last, has_above)
    pl.when(takes_below)(lambda: greet_halo(z - 1))
    pl.when(takes_above)(lambda: greet_halo(z + 1))
    pl.semaphore_wait(
        barrier,
        PEERS - 1 + jnp.where(has_below, 1, 0) + jnp.where(has_above, 1, 0),
    )

    def rows_of(to):
        return 48 * to - BELOW

    def copy_to(off, to, device, start, dst, size):
        return pltpu.make_async_remote_copy(
            src_ref=t_ref.at[pl.ds(start, size)],
            dst_ref=g_ref.at[place, pl.ds(dst, size)],
            send_sem=send_sem.at[off],
            recv_sem=recv_sem.at[off],
            device_id=device,
            device_id_type=MESH,
        )

    def three(to, act):
        pl.when(to == 0)(lambda: act(0, BELOW, WINDOW - BELOW))
        pl.when(to == PEERS - 1)(lambda: act(SEGMENT - BELOW - BINS, 0, BELOW + BINS))
        middle = jnp.logical_and(to > 0, to < PEERS - 1)
        pl.when(middle)(lambda: act(pl.multiple_of(48 * to - BELOW, 8), 0, WINDOW))

    def send(off, _):
        to, device = plane_peers(z, off, place)
        three(to, lambda start, dst, size: copy_to(off, to, device, start, dst, size).start())
        return 0

    lax.fori_loop(1, PEERS, send, 0)

    def halo_down():
        return pltpu.make_async_remote_copy(
            src_ref=t_ref.at[pl.ds(0, ABOVE)],
            dst_ref=g_ref.at[place, pl.ds(BELOW + BINS, ABOVE)],
            send_sem=halo_send.at[0],
            recv_sem=halo_recv.at[place],
            device_id=(8 * (z - 1) + 7, 3),
            device_id_type=MESH,
        )

    def halo_up():
        return pltpu.make_async_remote_copy(
            src_ref=t_ref.at[pl.ds(SEGMENT - BELOW, BELOW)],
            dst_ref=g_ref.at[place, pl.ds(0, BELOW)],
            send_sem=halo_send.at[1],
            recv_sem=halo_recv.at[place],
            device_id=(8 * (z + 1), 0),
            device_id_type=MESH,
        )

    pl.when(has_below)(lambda: halo_down().start())
    pl.when(has_above)(lambda: halo_up().start())

    def own(start, dst, size):
        copy = pltpu.make_async_copy(
            t_ref.at[pl.ds(start, size)], g_ref.at[place, pl.ds(dst, size)], own_sem
        )
        copy.start()
        copy.wait()

    three(place, own)

    def blank(dst, size):
        copy = pltpu.make_async_copy(
            zero_ref.at[:, pl.ds(0, size)], g_ref.at[:, pl.ds(dst, size)], zero_sem
        )
        copy.start()
        copy.wait()

    pl.when(jnp.logical_and(first, z == 0))(lambda: blank(0, BELOW))
    pl.when(jnp.logical_and(last, z == PLANES - 1))(lambda: blank(BELOW + BINS, ABOVE))

    def wait_send(off, _):
        to, device = plane_peers(z, off, place)
        three(to, lambda start, dst, size: copy_to(off, to, device, start, dst, size).wait_send())
        return 0

    def wait_recv(off, _):
        to, device = plane_peers(z, off, place)
        three(place, lambda start, dst, size: copy_to(off, to, device, start, dst, size).wait_recv())
        return 0

    lax.fori_loop(1, PEERS, wait_send, 0)
    lax.fori_loop(1, PEERS, wait_recv, 0)
    pl.when(has_below)(lambda: halo_down().wait_send())
    pl.when(has_above)(lambda: halo_up().wait_send())

    def wait_halo(dst, size):
        def body(index, _):
            pltpu.make_async_remote_copy(
                src_ref=t_ref.at[pl.ds(0, size)],
                dst_ref=g_ref.at[index, pl.ds(dst, size)],
                send_sem=halo_send.at[0],
                recv_sem=halo_recv.at[index],
                device_id=(pulse, lax.axis_index("rng")),
                device_id_type=MESH,
            ).wait_recv()
            return 0

        lax.fori_loop(0, PEERS, body, 0)

    pl.when(takes_below)(lambda: wait_halo(0, BELOW))
    pl.when(takes_above)(lambda: wait_halo(BELOW + BINS, ABOVE))


ANY = pl.BlockSpec(memory_space=pl.ANY)
WHOLE = pl.BlockSpec(memory_space=pltpu.VMEM)
SCALARS = pl.BlockSpec(memory_space=pltpu.SMEM)
DMA = pltpu.SemaphoreType.DMA


def params(collective=None, limit=40):
    extra = {} if collective is None else dict(collective_id=collective, has_side_effects=True)
    return pltpu.CompilerParams(vmem_limit_bytes=limit * 2**20, **extra)


def range_exchange(raw):
    tiles = raw.reshape(2, 2, 2, 4, 48, LANES).transpose(0, 1, 4, 2, 3, 5)
    return pl.pallas_call(
        range_exchange_kernel,
        out_shape=jax.ShapeDtypeStruct((2, ROWS, LANE_PULSES, LANES), F32),
        in_specs=[ANY],
        out_specs=ANY,
        scratch_shapes=[DMA((4,)), DMA((4,)), DMA],
        compiler_params=params(0),
    )(tiles)


def compress(x, range_filter):
    filt = range_filter.reshape(2, ROWS, LANES).transpose(1, 0, 2).reshape(2 * ROWS, LANES)
    order = filter_order()
    return pl.pallas_call(
        compress_kernel,
        out_shape=jax.ShapeDtypeStruct((PLANES * BLOCK, LANES), F32),
        in_specs=[WHOLE] * 7,
        out_specs=WHOLE,
        compiler_params=params(),
    )(
        x.reshape(2 * ROWS * LANE_PULSES, LANES),
        filt,
        table_first(),
        table_last(),
        table_twist(),
        right_factor(table_columns(np.arange(LANES), order, -1)),
        right_factor(table_columns(order, np.arange(LANES), 1)),
    )


def z_exchange(y):
    return pl.pallas_call(
        z_exchange_kernel,
        out_shape=jax.ShapeDtypeStruct(y.shape, F32),
        in_specs=[ANY],
        out_specs=ANY,
        scratch_shapes=[DMA((PLANES,)), DMA((PLANES,)), DMA],
        compiler_params=params(1),
    )(y)


def to_planes(z):
    table = table_planes()
    return pl.pallas_call(
        plane_kernel,
        out_shape=jax.ShapeDtypeStruct((SEGMENT, LANES), F32),
        in_specs=[WHOLE, ANY],
        out_specs=WHOLE,
        scratch_shapes=[pltpu.VMEM(table.shape[1:], BF16), DMA],
        compiler_params=params(),
    )(z, table)


def plane_exchange(t):
    return pl.pallas_call(
        plane_exchange_kernel,
        out_shape=jax.ShapeDtypeStruct((PEERS, WINDOW, LANES), F32),
        in_specs=[ANY, ANY],
        out_specs=ANY,
        scratch_shapes=[DMA((PEERS,)), DMA((PEERS,)), DMA((2,)), DMA((PEERS,)), DMA, DMA],
        compiler_params=params(2),
    )(t, np.zeros((PEERS, ABOVE, LANES), np.float32))


def by_bin(values):
    return values.reshape(16, 8, 16).transpose(2, 1, 0).reshape(16, LANES)


def azimuth(g, azimuth_filter, shifts, frac_index, kernel_table):
    return pl.pallas_call(
        azimuth_kernel,
        out_shape=jax.ShapeDtypeStruct((2, BINS, PULSES), F32),
        in_specs=[WHOLE] * 4 + [SCALARS] + [WHOLE] * 3,
        out_specs=WHOLE,
        scratch_shapes=[
            pltpu.VMEM((16, WINDOW, 2 * LANES), F32),
            pltpu.VMEM((2, WINDOW, LANES), F32),
            pltpu.VMEM((2, WINDOW, LANES), F32),
            pltpu.VMEM((2, 16, BINS, LANES), F32),
            pltpu.VMEM((2, 16, BINS, LANES), F32),
            pltpu.VMEM((TAPS, 16, LANES), F32),
        ],
        compiler_params=params(),
    )(
        g, azimuth_filter, by_bin(shifts), by_bin(frac_index), kernel_table,
        table_azimuth(), table_back(), table_back_twist(),
    )


def shards(raw, range_filter, azimuth_filter, shifts, frac_index, kernel_table):
    y = compress(range_exchange(raw), range_filter)
    g = plane_exchange(to_planes(z_exchange(y)))
    return azimuth(g, azimuth_filter, shifts, frac_index, kernel_table)


def solution(mesh):
    in_specs = (P(None, "pulse", "rng"), P(), P(None, ("pulse", "rng"), None), P(), P(), P())
    out_specs = P(None, ("pulse", "rng"), None)
    return jax.shard_map(shards, mesh=mesh, in_specs=in_specs, out_specs=out_specs, check_vma=False)
```

profile of v0, /device:TPU:1, one launch (start us, length us, event | category | flops | bytes accessed | tf_op | source)
XLA Modules:
  0.0 122.6 jit_solution(8011850963883642027)
XLA Ops:
  0.0 1.1 copy-done.4
  1.1 19.9 %shard_map.154 = f32[2,192,4,128]{3,2,1,0:T(4,128)S(1)} custom-call(f32[2,2,48,2,4,128]{5,4,3,2,1,0:T(4,128)S(1)} %bitcast.12), custom_call_target="tpu_custom_call" | custom-call | tf_op jit(solution)/shard_map/pallas_call | solution.py:510
  21.1 0.0 copy-start
  21.1 0.0 copy-start.1
  21.1 1.3 %copy-done.1 = bf16[384,1152]{1,0:T(8,128)(2,1)S(1)} copy-done((bf16[384,1152]{1,0:T(8,128)(2,1)S(1)}, bf16[384,1152]{1,0:T(8,128)(2,1)}, u32[]{:S(2)}) %copy-start.1) | copy-done | bytes 884760
  22.4 1.2 copy-done.2
  23.6 1.0 copy-done.7
  24.6 1.0 copy-done.8
  25.6 0.9 copy-done.9
  26.5 0.9 copy-done.10
  27.4 4.9 %shard_map.155.y_ref = f32[1536,128]{1,0:T(8,128)S(1)} custom-call(f32[1536,128]{1,0:T(8,128)S(1)} %bitcast.11, f32[384,128]{1,0:T(8,128)S(1)} %bitcast.13, bf16[384,1152]{1,0:T(8,128)(2,1)S(1)} %copy-done.1, bf16[384,1152]{1,0:T(8,128)(2,1)S(1)} %copy-done.2, f32[2,192,128]{2,1,0:T(8,128)S(1)} %copy-done.10, bf16[768,256]{1,0:T(8,128)(2,1)S(1)} %copy-done.7, ...), custom_call_target="tpu_custom_call" | custom-call | tf_op jit(solution)/shard_map/pallas_call | solution.py:523
  32.3 41.4 %shard_map.156.z_ref = f32[1536,128]{1,0:T(8,128)S(1)} custom-call(f32[1536,128]{1,0:T(8,128)S(1)} %shard_map.155.y_ref), custom_call_target="tpu_custom_call" | custom-call | tf_op jit(solution)/shard_map/pallas_call | solution.py:541
  73.7 0.0 copy-done
  73.7 0.0 copy-start.12
  73.7 0.0 copy-start.13
  73.7 0.0 copy-start.14
  73.7 0.0 copy-start.3
  73.8 0.0 copy-start.5
  73.8 0.0 copy-start.6
  73.8 0.0 copy-start.11
  73.8 3.1 %shard_map.157.t_ref = f32[1536,128]{1,0:T(8,128)S(1)} custom-call(f32[1536,128]{1,0:T(8,128)S(1)} %shard_map.156.z_ref, bf16[32,384,128]{2,1,0:T(8,128)(2,1)S(1)} %copy-done), custom_call_target="tpu_custom_call" | custom-call | tf_op jit(solution)/shard_map/pallas_call | solution.py:553
  76.9 30.3 %shard_map.158.g_ref = f32[32,80,128]{2,1,0:T(8,128)S(1)} custom-call(f32[1536,128]{1,0:T(8,128)S(1)} %shard_map.157.t_ref, f32[32,24,128]{2,1,0:T(8,128)S(1)} %jit_solution_.3.zero_ref), custom_call_target="tpu_custom_call" | custom-call | tf_op jit(solution)/shard_map/pallas_call | solution.py:564
  107.2 0.0 copy-done.12
  107.2 0.1 reshape.28
  107.3 0.1 copy.20
  107.4 0.1 reshape.29.shift_ref
  107.5 0.1 reshape.30
  107.6 0.1 copy.21
  107.7 0.1 reshape.31.frac_ref
  107.8 0.0 copy-done.14
  107.8 0.1 copy.22.ktab_ref
  107.9 14.7 %shard_map.159 = f32[2,48,2048]{2,1,0:T(8,128)} custom-call(f32[32,80,128]{2,1,0:T(8,128)S(1)} %shard_map.158.g_ref, f32[2,48,2048]{2,1,0:T(8,128)S(1)} %copy-done.3, s32[16,128]{1,0:T(8,128)S(1)} %reshape.29.shift_ref, s32[16,128]{1,0:T(8,128)S(1)} %reshape.31.frac_ref, f32[16,8]{1,0:T(8,128)S(1)} %copy.22.ktab_ref, bf16[768,256]{1,0:T(8,128)(2,1)S(1)} %copy-done.5, ...), custom_call_target="tpu_custom_call" | custom-call | tf_op jit(solution)/shard_map/pallas_call | solution.py:579
  (12 shorter events, 0.0 us)
Async XLA Ops:
  0.0 1.1 copy-start.4
  21.1 52.6 %copy-start = (bf16[32,384,128]{2,1,0:T(8,128)(2,1)S(1)}, bf16[32,384,128]{2,1,0:T(8,128)(2,1)}, u32[]{:S(2)}) copy-start(bf16[32,384,128]{2,1,0:T(8,128)(2,1)} %constant.25.clone.table_hbm) | copy-start | bytes 9437188
  21.1 1.3 %copy-start.1 = (bf16[384,1152]{1,0:T(8,128)(2,1)S(1)}, bf16[384,1152]{1,0:T(8,128)(2,1)}, u32[]{:S(2)}) copy-start(bf16[384,1152]{1,0:T(8,128)(2,1)} %constant.20.clone.first_ref) | copy-start | bytes 2654212
  22.4 1.2 copy-start.2
  23.6 1.0 copy-start.7
  24.6 1.0 copy-start.8
  25.6 0.9 copy-start.9
  26.5 0.9 copy-start.10
  73.7 33.5 %copy-start.12 = (s32[2048]{0:T(1024)S(1)}, s32[2048]{0:T(1024)}, u32[]{:S(2)}) copy-start(s32[2048]{0:T(1024)} %param.19) | copy-start | bytes 24580
  73.7 33.8 %copy-start.13 = (s32[2048]{0:T(1024)S(1)}, s32[2048]{0:T(1024)}, u32[]{:S(2)}) copy-start(s32[2048]{0:T(1024)} %param.20) | copy-start | bytes 24580
  73.7 34.0 %copy-start.14 = (f32[16,8]{0,1:T(8,128)S(1)}, f32[16,8]{0,1:T(8,128)}, u32[]{:S(2)}) copy-start(f32[16,8]{0,1:T(8,128)} %param.21) | copy-start | bytes 1540
  73.7 34.1 %copy-start.3 = (f32[2,48,2048]{2,1,0:T(8,128)S(1)}, f32[2,48,2048]{2,1,0:T(8,128)}, u32[]{:S(2)}) copy-start(f32[2,48,2048]{2,1,0:T(8,128)} %azf_ref.1) | copy-start | bytes 2359300
  73.8 34.1 %copy-start.5 = (bf16[768,256]{1,0:T(8,128)(2,1)S(1)}, bf16[768,256]{1,0:T(8,128)(2,1)}, u32[]{:S(2)}) copy-start(bf16[768,256]{1,0:T(8,128)(2,1)} %constant.27.clone.fwd_ref) | copy-start | bytes 1179652
  73.8 34.1 %copy-start.6 = (bf16[768,256]{1,0:T(8,128)(2,1)S(1)}, bf16[768,256]{1,0:T(8,128)(2,1)}, u32[]{:S(2)}) copy-start(bf16[768,256]{1,0:T(8,128)(2,1)} %constant.28.clone.back_ref) | copy-start | bytes 1179652
  73.8 34.1 %copy-start.11 = (f32[2,16,128]{2,1,0:T(8,128)S(1)}, f32[2,16,128]{2,1,0:T(8,128)}, u32[]{:S(2)}) copy-start(f32[2,16,128]{2,1,0:T(8,128)} %constant.29.clone.twist_ref) | copy-start | bytes 49156
where the time goes:
time: 123 us
  Pallas kernels  114 us (93%)
  local copies, waits for them, and re-layouts  8.12 us (7%)
    pallas_call x1, Pallas kernels, z_exchange(): pl.pallas_call(z_exchange_kernel, out_shape=jax.ShapeDtypeStruct(y.shape,...  41.4 us
    pallas_call x1, Pallas kernels, plane_exchange(): pl.pallas_call(plane_exchange_kernel, out_shape=jax.ShapeDtypeStruct((PEE...  30.3 us
    pallas_call x1, Pallas kernels, range_exchange(): pl.pallas_call(range_exchange_kernel, out_shape=jax.ShapeDtypeStruct((2,...  19.9 us
    pallas_call x1, Pallas kernels, azimuth(): pl.pallas_call(azimuth_kernel, out_shape=jax.ShapeDtypeStruct((2, BINS, P...  14.7 us
    unnamed x31, local copies, waits for them, and re-layouts  7.58 us
    pallas_call x1, Pallas kernels, compress(): pl.pallas_call(compress_kernel, out_shape=jax.ShapeDtypeStruct((PLANES *...  4.9 us
    pallas_call x1, Pallas kernels, to_planes(): pl.pallas_call(plane_kernel, out_shape=jax.ShapeDtypeStruct((SEGMENT, LAN...  3.05 us

commit v1 on v0

v1 whole, which is shorter than its diff:
```python
import functools
import math

import jax
import jax.numpy as jnp
import ml_dtypes
import numpy as np
from jax import lax
from jax.experimental import pallas as pl
from jax.experimental.pallas import tpu as pltpu
from jax.sharding import PartitionSpec as P

MESH = pl.DeviceIdType.MESH
F32 = jnp.float32
BF16 = jnp.bfloat16

PULSES = 2048
SAMPLES = 24576
ROWS = 192
LANES = 128
PLANES = 16
PEERS = 32
CHIPS = 16
LANE_PULSES = 4
BINS = 48
CHUNKS = 4
CHUNK_ROWS = 3
CHUNK = CHUNK_ROWS * LANES
PIECE = 2 * CHUNK_ROWS * LANE_PULSES
BELOW = 8
ABOVE = 24
WINDOW = BELOW + BINS + ABOVE
PAIR = BELOW + 2 * BINS + ABOVE
TAPS = 8
ORDER = (2, 1, 3, 0)


def turn(product, period, sign):
    angle = sign * 2.0 * math.pi * (product % period) / period
    return np.cos(angle), np.sin(angle)


def halves(table):
    high = table.astype(ml_dtypes.bfloat16)
    low = (table - high.astype(np.float64)).astype(ml_dtypes.bfloat16)
    return high, low


def left_factor(table):
    high, low = halves(table)
    return np.concatenate([high, high, low], axis=1)


def right_factor(table):
    high, low = halves(table)
    return np.concatenate([high, high, low], axis=-2)


def lane_bins():
    lanes = np.arange(LANES)
    return 8 * (lanes % 16) + lanes // 16


def table_first():
    ids = np.arange(ROWS)
    re, im = turn(np.outer(ids, ids), ROWS, -1)
    return left_factor(np.block([[re, -im], [im, re]]))


def table_last():
    ids = np.arange(ROWS)
    re, im = turn(np.outer(ids, ids), ROWS, 1)
    full = np.stack([np.concatenate([re, -im], axis=1), np.concatenate([im, re], axis=1)]) / SAMPLES
    full = full.reshape(2, PLANES, CHUNKS, CHUNK_ROWS, 2 * ROWS).transpose(2, 1, 0, 3, 4)
    return left_factor(full.reshape(2 * ROWS, 2 * ROWS)).reshape(CHUNKS, 2 * ROWS // CHUNKS, -1)


def filter_order():
    lanes = np.arange(LANES)
    return 2 * (lanes % 64) + lanes // 64


def table_columns(rows, cols, sign, scale=1.0):
    re, im = turn(np.outer(rows, cols), LANES, sign)
    return np.block([[re, im], [-im, re]]) * scale


def table_twist():
    re, im = turn(np.outer(np.arange(ROWS), np.arange(LANES)), SAMPLES, -1)
    return np.stack([re, im]).astype(np.float32)


def table_planes():
    place = np.arange(PEERS)[:, None, None, None]
    r = np.arange(LANE_PULSES)[None, :, None, None]
    z = np.arange(PLANES)[None, None, :, None]
    k1 = np.arange(16)[None, None, None, :]
    re, im = turn((128 * z + 4 * place + r) * k1, PULSES, -1)
    full = np.zeros((PEERS, 2, LANE_PULSES, PLANES, 16, 2, LANE_PULSES))
    for q in range(LANE_PULSES):
        full[:, 0, q, :, :, 0, q] = re[:, q]
        full[:, 1, q, :, :, 0, q] = -im[:, q]
        full[:, 0, q, :, :, 1, q] = im[:, q]
        full[:, 1, q, :, :, 1, q] = re[:, q]
    return right_factor(full.reshape(PEERS, 128, 128))


def table_azimuth():
    place = np.arange(PEERS)[:, None, None]
    r = np.arange(LANE_PULSES)[None, :, None]
    re, im = turn((4 * place + r) * lane_bins()[None, None, :], LANES, -1)
    full = np.zeros((PEERS, 2, LANE_PULSES, 2, LANES))
    full[:, 0, :, 0] = re
    full[:, 1, :, 0] = -im
    full[:, 0, :, 1] = im
    full[:, 1, :, 1] = re
    by_core = full.reshape(CHIPS, 2, 8, 2 * LANES).transpose(1, 0, 2, 3)
    return right_factor(by_core.reshape(2 * LANES, 2 * LANES))


def table_back():
    return right_factor(table_columns(lane_bins(), np.arange(LANES), 1, 1.0 / PULSES))


def table_back_twist():
    re, im = turn(np.outer(np.arange(16), np.arange(LANES)), PULSES, 1)
    return np.stack([re, im]).astype(np.float32)


def split(values):
    high = values.astype(BF16)
    low = (values - high.astype(F32)).astype(BF16)
    return high, low


def times_left(table, values):
    high, low = split(values)
    return jnp.dot(table, jnp.concatenate([high, low, high], axis=0), preferred_element_type=F32)


def times_right(values, table):
    high, low = split(values)
    return jnp.dot(jnp.concatenate([high, low, high], axis=1), table, preferred_element_type=F32)


def cmul(a_re, a_im, b_re, b_im):
    return a_re * b_re - a_im * b_im, a_re * b_im + a_im * b_re


def fft_list(values, sign):
    count = len(values)
    if count == 1:
        return values
    even = fft_list(values[0::2], sign)
    odd = fft_list(values[1::2], sign)
    low, high = [], []
    for k in range(count // 2):
        re, im = odd[k]
        if 4 * k == count:
            re, im = (-im, re) if sign > 0 else (im, -re)
        elif k:
            w_re = math.cos(2.0 * math.pi * k / count)
            w_im = sign * math.sin(2.0 * math.pi * k / count)
            re, im = re * w_re - im * w_im, re * w_im + im * w_re
        low.append((even[k][0] + re, even[k][1] + im))
        high.append((even[k][0] - re, even[k][1] - im))
    return low + high


def swap_blocks(arrays, width):
    arrays = list(arrays)
    lane = lax.broadcasted_iota(jnp.int32, arrays[0].shape, 1)
    for bit in (1, 2, 4, 8):
        keep = (lane // width) & bit == 0
        for a in range(16):
            if a & bit:
                continue
            first, second = arrays[a], arrays[a + bit]
            arrays[a] = jnp.where(keep, first, pltpu.roll(second, bit * width, 1))
            arrays[a + bit] = jnp.where(keep, pltpu.roll(first, LANES - bit * width, 1), second)
    return arrays


def kernel(
    raw_hbm, filt_hbm, azf_hbm, shift_hbm, frac_hbm, ktab_hbm,
    first_hbm, last_hbm, twist_hbm, fwd_hbm, back_hbm, planes_hbm, az_fwd_hbm, az_back_hbm, az_twist_hbm,
    out_ref,
    filt_in, azf_in, shift_in, frac_in, ktab, first, last, twist, fwd, back, planes, az_fwd, az_back, az_twist,
    load_sem,
    tiles, outgoing, x_ref, filt, v_ref, y_ref, z_ref, t_ref, g_ref, o_ref,
    shift_ref, w_ref, a_ref, h_ref, d_ref, e_ref, f_ref,
    tile_sem, x_send, x_recv, core_send, core_recv, z_send, z_recv, z_own,
    p_send, p_recv, h_send, h_recv, own_sem, halo_own, fwd_send, fwd_recv,
):
    pulse = lax.axis_index("pulse")
    lane = lax.axis_index("rng")
    z = lax.div(pulse, 8)
    y = lax.rem(lax.div(pulse, 2), 4)
    xh = lax.div(lane, 2)
    core = lax.rem(lane, 2)
    q_me = 2 * lax.rem(pulse, 2) + xh
    chip = 4 * y + q_me
    has_below = z > 0
    has_above = z < PLANES - 1

    def device(plane, other_chip, other_core):
        return (8 * plane + lax.div(other_chip, 2), 2 * lax.rem(other_chip, 2) + other_core)

    x_partner = (pulse, 2 * (1 - xh) + core)
    core_partner = (pulse, 2 * xh + 1 - core)

    barrier = pltpu.get_barrier_semaphore()

    def greet(to):
        pl.semaphore_signal(barrier, inc=1, device_id=to, device_id_type=MESH)

    greet(x_partner)
    greet(core_partner)

    def greet_z(off, _):
        greet(device(lax.rem(z + off, PLANES), chip, core))
        return 0

    def greet_plane(off, _):
        greet(device(z, lax.rem(chip + off, CHIPS), core))
        return 0

    def greet_all(plane):
        def body(other, _):
            greet(device(plane, other, core))
            return 0

        lax.fori_loop(0, CHIPS, body, 0)

    lax.fori_loop(1, PLANES, greet_z, 0)
    lax.fori_loop(1, CHIPS, greet_plane, 0)
    pl.when(jnp.logical_and(chip == 0, has_below))(lambda: greet_all(z - 1))
    pl.when(jnp.logical_and(chip == CHIPS - 1, has_above))(lambda: greet_all(z + 1))

    place = 2 * chip + core
    loads = [
        (filt_hbm, filt_in), (first_hbm, first), (twist_hbm, twist), (fwd_hbm, fwd), (back_hbm, back),
        (last_hbm, last), (planes_hbm.at[place], planes), (azf_hbm, azf_in), (shift_hbm, shift_in),
        (frac_hbm, frac_in), (ktab_hbm, ktab), (az_fwd_hbm, az_fwd), (az_back_hbm, az_back),
        (az_twist_hbm, az_twist),
    ]
    loads = [pltpu.make_async_copy(src, dst, load_sem.at[k]) for k, (src, dst) in enumerate(loads)]
    own_tiles = pltpu.make_async_copy(raw_hbm.at[:, xh], tiles.at[0], tile_sem)
    own_tiles.start()
    for load in loads:
        load.start()

    def blank(start, size):
        def body(other, _):
            g_ref[other, start : start + size, :] = jnp.zeros((size, LANES), F32)
            return 0

        lax.fori_loop(0, CHIPS, body, 0)

    pl.when(jnp.logical_and(chip == 0, z == 0))(lambda: blank(0, BELOW))
    pl.when(jnp.logical_and(chip == CHIPS - 1, z == PLANES - 1))(lambda: blank(PAIR - ABOVE, ABOVE))

    pl.semaphore_wait(
        barrier,
        2 + PLANES - 1 + CHIPS - 1 + jnp.where(has_below, 1, 0) + jnp.where(has_above, 1, 0),
    )

    to_x = pltpu.make_async_remote_copy(
        src_ref=raw_hbm.at[:, 1 - xh],
        dst_ref=tiles.at[1],
        send_sem=x_send,
        recv_sem=x_recv,
        device_id=x_partner,
        device_id_type=MESH,
    )
    to_x.start()

    def to_core(which):
        quarter = 2 * xh + core if which == 0 else 2 * (1 - xh) + core
        return pltpu.make_async_remote_copy(
            src_ref=outgoing.at[which],
            dst_ref=x_ref.at[:, :, pl.ds(pl.multiple_of(48 * quarter, 8), 48)],
            send_sem=core_send.at[which],
            recv_sem=core_recv.at[which],
            device_id=core_partner,
            device_id_type=MESH,
        )

    def sort_tiles(which):
        quarter = 2 * xh + core if which == 0 else 2 * (1 - xh) + core
        rows = pl.ds(pl.multiple_of(48 * quarter, 8), 48)
        for c in range(2):
            for r in range(LANE_PULSES):
                outgoing[which, c, r] = tiles[which, c, pl.ds(4 * (1 - core) + r, 48, stride=8), :]
        to_core(which).start()
        for c in range(2):
            for r in range(LANE_PULSES):
                x_ref[c, r, rows, :] = tiles[which, c, pl.ds(4 * core + r, 48, stride=8), :]

    own_tiles.wait()
    sort_tiles(0)

    for load in loads:
        load.wait()
    for c in range(2):
        cols = [filt_in[pl.ds(2 * u + c, 64, stride=6), :].T for u in range(3)]
        tall = jnp.concatenate(cols, axis=0)
        filt[c] = jnp.concatenate([tall[:ROWS], tall[ROWS:]], axis=1)

    to_x.wait_recv()
    sort_tiles(1)
    to_core(0).wait_recv()
    to_core(1).wait_recv()

    twist_re, twist_im = twist[0], twist[1]
    for half in range(2):
        pulses = (2 * half, 2 * half + 1)
        x = jnp.concatenate(
            [jnp.concatenate([x_ref[0, r], x_ref[1, r]], axis=0) for r in pulses], axis=1
        )
        v = times_left(first[...], x)
        rows = []
        for p in range(2):
            part = v[:, LANES * p : LANES * (p + 1)]
            rows.append(jnp.concatenate(cmul(part[:ROWS], part[ROWS:], twist_re, twist_im), axis=1))
        s = times_right(jnp.concatenate(rows, axis=0), fwd[...])
        rows = []
        for p in range(2):
            part = s[ROWS * p : ROWS * (p + 1)]
            rows.append(
                jnp.concatenate(cmul(part[:, :LANES], part[:, LANES:], filt[0], filt[1]), axis=1)
            )
        s = times_right(jnp.concatenate(rows, axis=0), back[...])
        for p in range(2):
            part = s[ROWS * p : ROWS * (p + 1)]
            turned = jnp.concatenate(
                cmul(part[:, :LANES], part[:, LANES:], twist_re, -twist_im), axis=0
            )
            high, low = split(turned)
            cols = slice(LANES * pulses[p], LANES * (pulses[p] + 1))
            v_ref[0 : 2 * ROWS, cols] = high
            v_ref[2 * ROWS : 4 * ROWS, cols] = low
            v_ref[4 * ROWS : 6 * ROWS, cols] = high

    def chunk_of(t):
        step = jnp.where(t == 0, ORDER[0], jnp.where(t == 1, ORDER[1], jnp.where(t == 2, ORDER[2], ORDER[3])))
        return lax.rem(y + step, CHUNKS)

    def z_copy(t, off):
        to = lax.rem(z + off, PLANES)
        return pltpu.make_async_remote_copy(
            src_ref=y_ref.at[t, to],
            dst_ref=z_ref.at[t, pl.ds(pl.multiple_of(PIECE * z, 8), PIECE)],
            send_sem=z_send.at[t, off],
            recv_sem=z_recv.at[t, off],
            device_id=device(to, chip, core),
            device_id_type=MESH,
        )

    def z_mine(t):
        return pltpu.make_async_copy(
            y_ref.at[t, z], z_ref.at[t, pl.ds(pl.multiple_of(PIECE * z, 8), PIECE)], z_own.at[t]
        )

    def send_chunk(t, _):
        out = jnp.dot(last[chunk_of(t)], v_ref[...], preferred_element_type=F32)
        size = 2 * CHUNK_ROWS
        for r in range(LANE_PULSES):
            for to in range(PLANES):
                y_ref[t, to, size * r : size * (r + 1), :] = out[
                    size * to : size * (to + 1), LANES * r : LANES * (r + 1)
                ]

        def start(near, _):
            z_copy(t, near).start()
            z_copy(t, PLANES - near).start()
            return 0

        z_copy(t, PLANES // 2).start()
        lax.fori_loop(1, PLANES // 2, start, 0)
        z_mine(t).start()
        return 0

    lax.fori_loop(0, CHUNKS, send_chunk, 0)

    def turn_filter(step, _):
        rows = pl.ds(pl.multiple_of(8 * step, 8), 8)
        for c in range(2):
            got = swap_blocks([azf_in[c, rows, LANES * k : LANES * (k + 1)] for k in range(16)], 1)
            for k1 in range(16):
                a_ref[c, k1, rows, :] = got[k1]
        return 0

    lax.fori_loop(0, BINS // 8, turn_filter, 0)

    def by_bin(values):
        tall = values.T
        return jnp.concatenate([tall[16 * u : 16 * (u + 1)] for u in range(8)], axis=1)

    shift_ref[...] = by_bin(shift_in[...])
    frac = by_bin(frac_in[...])
    for tap in range(TAPS):
        weight = jnp.zeros(frac.shape, F32)
        for row in range(16):
            weight = jnp.where(frac == row, ktab[tap, row], weight)
        w_ref[tap] = weight

    def main_copy(t, q, src, dst, size):
        return pltpu.make_async_remote_copy(
            src_ref=t_ref.at[t, pl.ds(src, size)],
            dst_ref=g_ref.at[chip, pl.ds(dst, size)],
            send_sem=p_send.at[t, q],
            recv_sem=p_recv.at[chip],
            device_id=device(z, 4 * chunk_of(t) + q, core),
            device_id_type=MESH,
        )

    def main_recv(other, src, dst, size):
        return pltpu.make_async_remote_copy(
            src_ref=t_ref.at[0, pl.ds(src, size)],
            dst_ref=g_ref.at[other, pl.ds(dst, size)],
            send_sem=p_send.at[0, 0],
            recv_sem=p_recv.at[other],
            device_id=core_partner,
            device_id_type=MESH,
        )

    def main_own(src, dst, size):
        return pltpu.make_async_copy(
            t_ref.at[CHUNKS - 1, pl.ds(src, size)], g_ref.at[chip, pl.ds(dst, size)], own_sem
        )

    def windows(q, act):
        pl.when(q == 0)(lambda: act(0, BELOW, PAIR - BELOW))
        pl.when(q == 3)(lambda: act(CHUNK - BELOW - 2 * BINS, 0, PAIR - ABOVE))
        middle = jnp.logical_and(q > 0, q < 3)
        pl.when(middle)(lambda: act(pl.multiple_of(2 * BINS * q - BELOW, 8), 0, PAIR))

    def halo_targets(chunk):
        down_chip = lax.rem(4 * chunk + CHIPS - 1, CHIPS)
        up_chip = lax.rem(4 * chunk + 4, CHIPS)
        down_plane = jnp.where(chunk == 0, z - 1, z)
        up_plane = jnp.where(chunk == CHUNKS - 1, z + 1, z)
        return down_plane, down_chip, up_plane, up_chip

    DOWN = (0, PAIR - ABOVE, ABOVE)
    UP = (CHUNK - BELOW, 0, BELOW)

    def halo_copy(t, which, plane, to):
        src, dst, size = (DOWN, UP)[which]
        return pltpu.make_async_remote_copy(
            src_ref=t_ref.at[t, pl.ds(src, size)],
            dst_ref=g_ref.at[chip, pl.ds(dst, size)],
            send_sem=h_send.at[t, which],
            recv_sem=h_recv.at[chip],
            device_id=device(plane, to, core),
            device_id_type=MESH,
        )

    def halo_mine(t, which):
        src, dst, size = (DOWN, UP)[which]
        return pltpu.make_async_copy(
            t_ref.at[t, pl.ds(src, size)], g_ref.at[chip, pl.ds(dst, size)], halo_own
        )

    def halo_recv(other, which):
        src, dst, size = (DOWN, UP)[which]
        return pltpu.make_async_remote_copy(
            src_ref=t_ref.at[0, pl.ds(src, size)],
            dst_ref=g_ref.at[other, pl.ds(dst, size)],
            send_sem=h_send.at[0, which],
            recv_sem=h_recv.at[other],
            device_id=core_partner,
            device_id_type=MESH,
        )

    def each_halo(t, remote, local):
        down_plane, down_chip, up_plane, up_chip = halo_targets(chunk_of(t))
        for which, plane, to in ((0, down_plane, down_chip), (1, up_plane, up_chip)):
            inside = jnp.logical_and(plane >= 0, plane < PLANES)
            me = jnp.logical_and(plane == z, to == chip)
            pl.when(jnp.logical_and(inside, jnp.logical_not(me)))(
                functools.partial(remote, t, which, plane, to)
            )
            pl.when(me)(functools.partial(local, t, which))

    def each_main(t, act):
        for off in range(4):
            q = lax.rem(q_me + off, 4)
            to_me = jnp.logical_and(t == CHUNKS - 1, off == 0)

            def remote(q=q):
                windows(q, functools.partial(act, t, q))

            pl.when(jnp.logical_not(to_me))(remote)

    def plane_step(t, _):
        def wait_z(off, _):
            z_copy(t, off).wait_recv()
            return 0

        lax.fori_loop(1, PLANES, wait_z, 0)
        z_mine(t).wait()
        for row in range(CHUNK_ROWS):
            parts = []
            for c in range(2):
                for r in range(LANE_PULSES):
                    start = CHUNK_ROWS * (2 * r + c) + row
                    parts.append(z_ref[t, pl.ds(start, PLANES, stride=PIECE), :])
            t_ref[t, LANES * row : LANES * (row + 1), :] = times_right(
                jnp.concatenate(parts, axis=0).T, planes[...]
            )
        each_main(t, lambda *a: main_copy(*a).start())

        def local(t, which):
            halo_mine(t, which).start()
            halo_mine(t, which).wait()

        each_halo(t, lambda *a: halo_copy(*a).start(), local)
        return 0

    lax.fori_loop(0, CHUNKS, plane_step, 0)

    def own(src, dst, size):
        main_own(src, dst, size).start()
        main_own(src, dst, size).wait()

    windows(q_me, own)

    def core_copy(row):
        return pltpu.make_async_remote_copy(
            src_ref=g_ref.at[pl.ds(4 * row, 4), pl.ds(pl.multiple_of(BINS * (1 - core), 8), WINDOW)],
            dst_ref=o_ref.at[pl.ds(4 * row, 4)],
            send_sem=fwd_send.at[row],
            recv_sem=fwd_recv.at[row],
            device_id=core_partner,
            device_id_type=MESH,
        )

    takes_up = jnp.logical_and(q_me == 0, jnp.logical_or(y > 0, has_below))
    takes_down = jnp.logical_and(q_me == 3, jnp.logical_or(y < 3, has_above))
    other_plane = jnp.where(q_me == 0, y == 0, y == 3)

    def gather(t, _):
        row = lax.rem(y + CHUNKS - chunk_of(t) + y, CHUNKS)

        def one(k, _):
            other = 4 * row + k
            mine = other == chip
            pl.when(jnp.logical_not(mine))(
                lambda: windows(q_me, lambda *a: main_recv(other, *a).wait_recv())
            )
            remote = jnp.logical_or(other_plane, jnp.logical_not(mine))
            pl.when(jnp.logical_and(takes_up, remote))(lambda: halo_recv(other, 1).wait_recv())
            pl.when(jnp.logical_and(takes_down, remote))(lambda: halo_recv(other, 0).wait_recv())
            return 0

        lax.fori_loop(0, 4, one, 0)
        core_copy(row).start()
        return 0

    lax.fori_loop(0, CHUNKS, gather, 0)

    def turn_own(step, _):
        rows = pl.ds(pl.multiple_of(8 * step, 8), 8)
        start = pl.ds(pl.multiple_of(BINS * core + 8 * step, 8), 8)
        got = swap_blocks([g_ref[k, start, :] for k in range(CHIPS)], 8)
        for k1 in range(16):
            h_ref[core, k1, rows, :] = got[k1]
        return 0

    def turn_other(step, _):
        rows = pl.ds(pl.multiple_of(8 * step, 8), 8)
        got = swap_blocks([o_ref[k, rows, :] for k in range(CHIPS)], 8)
        for k1 in range(16):
            h_ref[1 - core, k1, rows, :] = got[k1]
        return 0

    lax.fori_loop(0, WINDOW // 8, turn_own, 0)

    def wait_core(row, _):
        core_copy(row).wait_recv()
        return 0

    lax.fori_loop(0, 4, wait_core, 0)
    lax.fori_loop(0, WINDOW // 8, turn_other, 0)

    def per_bin(k1, _):
        d = times_right(jnp.concatenate([h_ref[0, k1], h_ref[1, k1]], axis=1), az_fwd[...])
        shift = shift_ref[pl.ds(k1, 1), :]
        weights = [w_ref[tap, pl.ds(k1, 1), :] for tap in range(TAPS)]
        moved = []
        for c in range(2):
            x = d[:, LANES * c : LANES * (c + 1)]
            near = jnp.where((shift & 16) != 0, x[16:80], x[0:64])
            x = jnp.concatenate([near, x[64:80]], axis=0)
            d_ref[c, 0:72] = jnp.where((shift & 8) != 0, x[8:80], x[0:72])
            e_ref[c, 0:64] = jnp.where((shift & 4) != 0, d_ref[c, 4:68], d_ref[c, 0:64])
            d_ref[c, 0:62] = jnp.where((shift & 2) != 0, e_ref[c, 2:64], e_ref[c, 0:62])
            e_ref[c, 0:61] = jnp.where((shift & 1) != 0, d_ref[c, 1:62], d_ref[c, 0:61])
            total = weights[0] * e_ref[c, 5 : 5 + BINS]
            for tap in range(1, TAPS):
                total = total + weights[tap] * e_ref[c, 5 + tap : 5 + tap + BINS]
            moved.append(total)
        re, im = cmul(moved[0], moved[1], a_ref[0, k1], a_ref[1, k1])
        s = times_right(jnp.concatenate([re, im], axis=1), az_back[...])
        re, im = cmul(
            s[:, :LANES], s[:, LANES:], az_twist[0, pl.ds(k1, 1), :], az_twist[1, pl.ds(k1, 1), :]
        )
        f_ref[0, k1] = re
        f_ref[1, k1] = im
        return 0

    lax.fori_loop(0, 16, per_bin, 0)

    def finish(step, _):
        rows = pl.ds(pl.multiple_of(8 * step, 8), 8)
        got = fft_list([(f_ref[0, k1, rows, :], f_ref[1, k1, rows, :]) for k1 in range(16)], 1)
        for tile in range(16):
            out_ref[0, rows, LANES * tile : LANES * (tile + 1)] = got[tile][0]
            out_ref[1, rows, LANES * tile : LANES * (tile + 1)] = got[tile][1]
        return 0

    lax.fori_loop(0, BINS // 8, finish, 0)

    to_x.wait_send()
    to_core(0).wait_send()
    to_core(1).wait_send()

    def wait_sends(t, _):
        def wait_z_send(off, _):
            z_copy(t, off).wait_send()
            return 0

        lax.fori_loop(1, PLANES, wait_z_send, 0)
        each_main(t, lambda *a: main_copy(*a).wait_send())
        each_halo(t, lambda *a: halo_copy(*a).wait_send(), lambda *a: None)
        core_copy(t).wait_send()
        return 0

    lax.fori_loop(0, CHUNKS, wait_sends, 0)


ANY = pl.BlockSpec(memory_space=pl.ANY)
DMA = pltpu.SemaphoreType.DMA


def shards(raw, range_filter, azimuth_filter, shifts, frac_index, kernel_table):
    order = filter_order()
    tables = [
        table_first(),
        table_last(),
        table_twist(),
        right_factor(table_columns(np.arange(LANES), order, -1)),
        right_factor(table_columns(order, np.arange(LANES), 1)),
        table_planes(),
        table_azimuth(),
        table_back(),
        table_back_twist(),
    ]
    operands = [
        raw.reshape(2, 2, 8, 48, LANES).transpose(0, 1, 3, 2, 4).reshape(2, 2, 384, LANES),
        range_filter.reshape(2, ROWS, LANES).transpose(1, 0, 2).reshape(2 * ROWS, LANES),
        azimuth_filter,
        shifts.reshape(16, LANES),
        frac_index.reshape(16, LANES),
        kernel_table.T,
    ]

    def like(array, shape=None):
        return pltpu.VMEM(array.shape if shape is None else shape, array.dtype)

    loads = [like(a) for a in operands[1:5]] + [pltpu.SMEM(operands[5].shape, F32)]
    loads += [like(a) for a in tables]
    loads[5 + 5] = like(tables[5], tables[5].shape[1:])
    scratch = [
        pltpu.VMEM((2, 2, 384, LANES), F32),
        pltpu.VMEM((2, 2, LANE_PULSES, 48, LANES), F32),
        pltpu.VMEM((2, LANE_PULSES, ROWS, LANES), F32),
        pltpu.VMEM((2, ROWS, LANES), F32),
        pltpu.VMEM((6 * ROWS, LANE_PULSES * LANES), BF16),
        pltpu.VMEM((CHUNKS, PLANES, PIECE, LANES), F32),
        pltpu.VMEM((CHUNKS, PLANES * PIECE, LANES), F32),
        pltpu.VMEM((CHUNKS, CHUNK, LANES), F32),
        pltpu.VMEM((CHIPS, PAIR, LANES), F32),
        pltpu.VMEM((CHIPS, WINDOW, LANES), F32),
        pltpu.VMEM((16, LANES), jnp.int32),
        pltpu.VMEM((TAPS, 16, LANES), F32),
        pltpu.VMEM((2, 16, BINS, LANES), F32),
        pltpu.VMEM((2, 16, WINDOW, LANES), F32),
        pltpu.VMEM((2, WINDOW, LANES), F32),
        pltpu.VMEM((2, WINDOW, LANES), F32),
        pltpu.VMEM((2, 16, BINS, LANES), F32),
        DMA, DMA, DMA, DMA((2,)), DMA((2,)),
        DMA((CHUNKS, PLANES)), DMA((CHUNKS, PLANES)), DMA((CHUNKS,)),
        DMA((CHUNKS, 4)), DMA((CHIPS,)), DMA((CHUNKS, 2)), DMA((CHIPS,)), DMA, DMA, DMA((4,)), DMA((4,)),
    ]
    return pl.pallas_call(
        kernel,
        out_shape=jax.ShapeDtypeStruct((2, BINS, PULSES), F32),
        in_specs=[ANY] * (len(operands) + len(tables)),
        out_specs=pl.BlockSpec(memory_space=pltpu.VMEM),
        scratch_shapes=loads + [DMA((len(loads),))] + scratch,
        compiler_params=pltpu.CompilerParams(
            vmem_limit_bytes=60 * 2**20, collective_id=0, has_side_effects=True
        ),
    )(*operands, *tables)


def solution(mesh):
    in_specs = (P(None, "pulse", "rng"), P(), P(None, ("pulse", "rng"), None), P(), P(), P())
    out_specs = P(None, ("pulse", "rng"), None)
    return jax.shard_map(shards, mesh=mesh, in_specs=in_specs, out_specs=out_specs, check_vma=False)
```

time: 123 us -> 94.2 us (0.77)
  Pallas kernels: 114 us -> 91.9 us
  local copies, waits for them, and re-layouts: 8.12 us -> 2.06 us
    pallas_call x6 -> x1, Pallas kernels: 114 us -> 91.9 us  [shards(): pl.pallas_call(kernel, out_shape=jax.ShapeDtypeStruct((2, BINS, PULSES),...]
    unnamed x31 -> x1, local copies, waits for them, and re-layouts: 7.58 us -> 2.06 us
where the time goes in v1:
time: 94.2 us; the launch traced here: 94 us
  Pallas kernels  91.9 us (98%)
  local copies, waits for them, and re-layouts  2.06 us (2%)
    pallas_call x1, Pallas kernels, shards(): pl.pallas_call(kernel, out_shape=jax.ShapeDtypeStruct((2, BINS, PULSES),...  91.9 us
    unnamed x1, local copies, waits for them, and re-layouts  2.06 us

profile of v1, /device:TPU:1, one launch (start us, length us, event | category | flops | bytes accessed | tf_op | source)
XLA Modules:
  0.0 94.0 jit_solution(11750087127300315834)
XLA Ops:
  0.0 91.9 %shard_map.145 = f32[2,48,2048]{2,1,0:T(8,128)} custom-call(f32[2,2,384,128]{3,2,1,0:T(8,128)} %bitcast.13, f32[384,128]{1,0:T(8,128)} %bitcast.14, f32[2,48,2048]{2,1,0:T(8,128)} %azf_hbm.1, s32[16,128]{1,0:T(8,128)} %bitcast.15, s32[16,128]{1,0:T(8,128)} %bitcast.16, f32[8,16]{1,0:T(8,128)} %bitcast.17, bf16[384,1152]{1,0:T(8,128)(2,1)} %constant.18.clone.first_hbm, ...), custom_call_target="tpu_custom_call" | custom-call | tf_op jit(solution)/shard_map/pallas_call | solution.py:698
  91.9 2.1 %copy.18 = f32[2,48,2048]{2,1,0:T(8,128)} copy(f32[2,48,2048]{2,1,0:T(8,128)} %shard_map.145) | data formatting | bytes 1572864

commit v2 on v1

--- a/solution.py
+++ b/solution.py
@@ -115,7 +115,7 @@
     full[:, 0, :, 1] = im
     full[:, 1, :, 1] = re
     by_core = full.reshape(CHIPS, 2, 8, 2 * LANES).transpose(1, 0, 2, 3)
-    return right_factor(by_core.reshape(2 * LANES, 2 * LANES))
+    return right_factor(by_core.reshape(2, LANES, 2 * LANES))
 
 
 def table_back():
@@ -187,8 +187,8 @@
     out_ref,
     filt_in, azf_in, shift_in, frac_in, ktab, first, last, twist, fwd, back, planes, az_fwd, az_back, az_twist,
     load_sem,
-    tiles, outgoing, x_ref, filt, v_ref, y_ref, z_ref, t_ref, g_ref, o_ref,
-    shift_ref, w_ref, a_ref, h_ref, d_ref, e_ref, f_ref,
+    tiles, to_like, to_relay, relay, to_core, x_ref, filt, v_ref, y_ref, z_ref, t_ref, g_ref, o_ref,
+    shift_ref, w_ref, a_ref, h_ref, d_ref, m_ref, e_ref, f_ref,
     tile_sem, x_send, x_recv, core_send, core_recv, z_send, z_recv, z_own,
     p_send, p_recv, h_send, h_recv, own_sem, halo_own, fwd_send, fwd_recv,
 ):
@@ -245,9 +245,11 @@
         (az_twist_hbm, az_twist),
     ]
     loads = [pltpu.make_async_copy(src, dst, load_sem.at[k]) for k, (src, dst) in enumerate(loads)]
-    own_tiles = pltpu.make_async_copy(raw_hbm.at[:, xh], tiles.at[0], tile_sem)
-    own_tiles.start()
-    for load in loads:
+    tile_loads = [
+        pltpu.make_async_copy(raw_hbm.at[:, 1 - xh], tiles.at[1], tile_sem.at[1]),
+        pltpu.make_async_copy(raw_hbm.at[:, xh], tiles.at[0], tile_sem.at[0]),
+    ]
+    for load in tile_loads + loads:
         load.start()
 
     def blank(start, size):
@@ -260,45 +262,53 @@
     pl.when(jnp.logical_and(chip == 0, z == 0))(lambda: blank(0, BELOW))
     pl.when(jnp.logical_and(chip == CHIPS - 1, z == PLANES - 1))(lambda: blank(PAIR - ABOVE, ABOVE))
 
+    my_quarter = 2 * xh + core
+    x_quarter = 2 * (1 - xh) + core
+
+    def quarter_rows(quarter):
+        return pl.ds(pl.multiple_of(48 * quarter, 8), 48)
+
+    for load in tile_loads:
+        load.wait()
+    for r in range(LANE_PULSES):
+        like = pl.ds(4 * core + r, 48, stride=8)
+        other = pl.ds(4 * (1 - core) + r, 48, stride=8)
+        for c in range(2):
+            to_like[r, c] = tiles[1, c, like, :]
+            to_relay[r, c] = tiles[1, c, other, :]
+            to_core[r, c] = tiles[0, c, other, :]
+            x_ref[r, c, quarter_rows(my_quarter), :] = tiles[0, c, like, :]
+
     pl.semaphore_wait(
         barrier,
         2 + PLANES - 1 + CHIPS - 1 + jnp.where(has_below, 1, 0) + jnp.where(has_above, 1, 0),
     )
 
-    to_x = pltpu.make_async_remote_copy(
-        src_ref=raw_hbm.at[:, 1 - xh],
-        dst_ref=tiles.at[1],
-        send_sem=x_send,
-        recv_sem=x_recv,
-        device_id=x_partner,
-        device_id_type=MESH,
-    )
-    to_x.start()
-
-    def to_core(which):
-        quarter = 2 * xh + core if which == 0 else 2 * (1 - xh) + core
+    def x_copy(r, which):
         return pltpu.make_async_remote_copy(
-            src_ref=outgoing.at[which],
-            dst_ref=x_ref.at[:, :, pl.ds(pl.multiple_of(48 * quarter, 8), 48)],
-            send_sem=core_send.at[which],
-            recv_sem=core_recv.at[which],
+            src_ref=(to_like, to_relay)[which].at[r],
+            dst_ref=x_ref.at[r, :, quarter_rows(my_quarter)] if which == 0 else relay.at[r],
+            send_sem=x_send.at[r, which],
+            recv_sem=x_recv.at[r, which],
+            device_id=x_partner,
+            device_id_type=MESH,
+        )
+
+    def core_swap(r, which):
+        return pltpu.make_async_remote_copy(
+            src_ref=(to_core, relay)[which].at[r],
+            dst_ref=x_ref.at[r, :, quarter_rows((my_quarter, x_quarter)[which])],
+            send_sem=core_send.at[r, which],
+            recv_sem=core_recv.at[r, which],
             device_id=core_partner,
             device_id_type=MESH,
         )
 
-    def sort_tiles(which):
-        quarter = 2 * xh + core if which == 0 else 2 * (1 - xh) + core
-        rows = pl.ds(pl.multiple_of(48 * quarter, 8), 48)
-        for c in range(2):
-            for r in range(LANE_PULSES):
-                outgoing[which, c, r] = tiles[which, c, pl.ds(4 * (1 - core) + r, 48, stride=8), :]
-        to_core(which).start()
-        for c in range(2):
-            for r in range(LANE_PULSES):
-                x_ref[c, r, rows, :] = tiles[which, c, pl.ds(4 * core + r, 48, stride=8), :]
-
-    own_tiles.wait()
-    sort_tiles(0)
+    for r in range(LANE_PULSES):
+        x_copy(r, 1).start()
+        x_copy(r, 0).start()
+    for r in range(LANE_PULSES):
+        core_swap(r, 0).start()
 
     for load in loads:
         load.wait()
@@ -307,81 +317,85 @@
         tall = jnp.concatenate(cols, axis=0)
         filt[c] = jnp.concatenate([tall[:ROWS], tall[ROWS:]], axis=1)
 
-    to_x.wait_recv()
-    sort_tiles(1)
-    to_core(0).wait_recv()
-    to_core(1).wait_recv()
-
-    twist_re, twist_im = twist[0], twist[1]
-    for half in range(2):
-        pulses = (2 * half, 2 * half + 1)
-        x = jnp.concatenate(
-            [jnp.concatenate([x_ref[0, r], x_ref[1, r]], axis=0) for r in pulses], axis=1
-        )
-        v = times_left(first[...], x)
-        rows = []
-        for p in range(2):
-            part = v[:, LANES * p : LANES * (p + 1)]
-            rows.append(jnp.concatenate(cmul(part[:ROWS], part[ROWS:], twist_re, twist_im), axis=1))
-        s = times_right(jnp.concatenate(rows, axis=0), fwd[...])
-        rows = []
-        for p in range(2):
-            part = s[ROWS * p : ROWS * (p + 1)]
-            rows.append(
-                jnp.concatenate(cmul(part[:, :LANES], part[:, LANES:], filt[0], filt[1]), axis=1)
-            )
-        s = times_right(jnp.concatenate(rows, axis=0), back[...])
-        for p in range(2):
-            part = s[ROWS * p : ROWS * (p + 1)]
-            turned = jnp.concatenate(
-                cmul(part[:, :LANES], part[:, LANES:], twist_re, -twist_im), axis=0
-            )
-            high, low = split(turned)
-            cols = slice(LANES * pulses[p], LANES * (pulses[p] + 1))
-            v_ref[0 : 2 * ROWS, cols] = high
-            v_ref[2 * ROWS : 4 * ROWS, cols] = low
-            v_ref[4 * ROWS : 6 * ROWS, cols] = high
+    def compress(r):
+        x_copy(r, 1).wait_recv()
+        core_swap(r, 1).start()
+        x_copy(r, 0).wait_recv()
+        core_swap(r, 0).wait_recv()
+        core_swap(r, 1).wait_recv()
+        twist_re, twist_im = twist[0], twist[1]
+        v = times_left(first[...], jnp.concatenate([x_ref[r, 0], x_ref[r, 1]], axis=0))
+        re, im = cmul(v[:ROWS], v[ROWS:], twist_re, twist_im)
+        s = times_right(jnp.concatenate([re, im], axis=1), fwd[...])
+        re, im = cmul(s[:, :LANES], s[:, LANES:], filt[0], filt[1])
+        s = times_right(jnp.concatenate([re, im], axis=1), back[...])
+        re, im = cmul(s[:, :LANES], s[:, LANES:], twist_re, -twist_im)
+        high, low = split(jnp.concatenate([re, im], axis=0))
+        v_ref[r, 0 : 2 * ROWS] = high
+        v_ref[r, 2 * ROWS : 4 * ROWS] = low
+        v_ref[r, 4 * ROWS : 6 * ROWS] = high
 
     def chunk_of(t):
         step = jnp.where(t == 0, ORDER[0], jnp.where(t == 1, ORDER[1], jnp.where(t == 2, ORDER[2], ORDER[3])))
         return lax.rem(y + step, CHUNKS)
 
-    def z_copy(t, off):
+    def z_copy(block, off):
         to = lax.rem(z + off, PLANES)
         return pltpu.make_async_remote_copy(
-            src_ref=y_ref.at[t, to],
-            dst_ref=z_ref.at[t, pl.ds(pl.multiple_of(PIECE * z, 8), PIECE)],
-            send_sem=z_send.at[t, off],
-            recv_sem=z_recv.at[t, off],
+            src_ref=y_ref.at[block, to],
+            dst_ref=z_ref.at[block, pl.ds(pl.multiple_of(PIECE * z, 8), PIECE)],
+            send_sem=z_send.at[block, off],
+            recv_sem=z_recv.at[block, off],
             device_id=device(to, chip, core),
             device_id_type=MESH,
         )
 
-    def z_mine(t):
+    def z_mine(block):
         return pltpu.make_async_copy(
-            y_ref.at[t, z], z_ref.at[t, pl.ds(pl.multiple_of(PIECE * z, 8), PIECE)], z_own.at[t]
-        )
-
-    def send_chunk(t, _):
-        out = jnp.dot(last[chunk_of(t)], v_ref[...], preferred_element_type=F32)
-        size = 2 * CHUNK_ROWS
-        for r in range(LANE_PULSES):
+            y_ref.at[block, z], z_ref.at[block, pl.ds(pl.multiple_of(PIECE * z, 8), PIECE)], z_own.at[block]
+        )
+
+    def send_block(block):
+        def start(near, _):
+            z_copy(block, near).start()
+            z_copy(block, PLANES - near).start()
+            return 0
+
+        z_copy(block, PLANES // 2).start()
+        lax.fori_loop(1, PLANES // 2, start, 0)
+        z_mine(block).start()
+
+    size = 2 * CHUNK_ROWS
+
+    def one_pulse(r, _):
+        compress(r)
+        for chunk in range(CHUNKS):
+            out = jnp.dot(last[chunk], v_ref[r], preferred_element_type=F32)
             for to in range(PLANES):
-                y_ref[t, to, size * r : size * (r + 1), :] = out[
-                    size * to : size * (to + 1), LANES * r : LANES * (r + 1)
-                ]
-
-        def start(near, _):
-            z_copy(t, near).start()
-            z_copy(t, PLANES - near).start()
-            return 0
-
-        z_copy(t, PLANES // 2).start()
-        lax.fori_loop(1, PLANES // 2, start, 0)
-        z_mine(t).start()
-        return 0
-
-    lax.fori_loop(0, CHUNKS, send_chunk, 0)
+                y_ref[r, to, size * chunk : size * (chunk + 1), :] = out[size * to : size * (to + 1)]
+        send_block(r)
+        return 0
+
+    def two_chunks(pair, _):
+        both = jnp.concatenate([v_ref[2], v_ref[3]], axis=1)
+        for half in range(2):
+            out = jnp.dot(last[chunk_of(2 * pair + half)], both, preferred_element_type=F32)
+            for r in range(2):
+                place = size * (2 * half + r)
+                for to in range(PLANES):
+                    y_ref[2 + pair, to, place : place + size, :] = out[
+                        size * to : size * (to + 1), LANES * r : LANES * (r + 1)
+                    ]
+        send_block(2 + pair)
+        return 0
+
+    def later_pulse(r, _):
+        compress(r)
+        return 0
+
+    lax.fori_loop(0, 2, one_pulse, 0)
+    lax.fori_loop(2, 4, later_pulse, 0)
+    lax.fori_loop(0, 2, two_chunks, 0)
 
     def turn_filter(step, _):
         rows = pl.ds(pl.multiple_of(8 * step, 8), 8)
@@ -494,19 +508,36 @@
 
             pl.when(jnp.logical_not(to_me))(remote)
 
+    def wait_block(block, _):
+        def wait_z(off, _):
+            z_copy(block, off).wait_recv()
+            return 0
+
+        lax.fori_loop(1, PLANES, wait_z, 0)
+        z_mine(block).wait()
+        return 0
+
     def plane_step(t, _):
-        def wait_z(off, _):
-            z_copy(t, off).wait_recv()
-            return 0
-
-        lax.fori_loop(1, PLANES, wait_z, 0)
-        z_mine(t).wait()
+        @pl.when(t == 0)
+        def _():
+            lax.fori_loop(0, 3, wait_block, 0)
+
+        @pl.when(t == 2)
+        def _():
+            wait_block(3, 0)
+
+        pair = lax.div(t, 2)
+        half = lax.rem(t, 2)
+        chunk = chunk_of(t)
         for row in range(CHUNK_ROWS):
             parts = []
             for c in range(2):
-                for r in range(LANE_PULSES):
-                    start = CHUNK_ROWS * (2 * r + c) + row
-                    parts.append(z_ref[t, pl.ds(start, PLANES, stride=PIECE), :])
+                for r in range(2):
+                    start = size * chunk + CHUNK_ROWS * c + row
+                    parts.append(z_ref[r, pl.ds(start, PLANES, stride=PIECE), :])
+                for r in range(2):
+                    start = size * (2 * half + r) + CHUNK_ROWS * c + row
+                    parts.append(z_ref[2 + pair, pl.ds(start, PLANES, stride=PIECE), :])
             t_ref[t, LANES * row : LANES * (row + 1), :] = times_right(
                 jnp.concatenate(parts, axis=0).T, planes[...]
             )
@@ -561,57 +592,77 @@
 
     lax.fori_loop(0, CHUNKS, gather, 0)
 
-    def turn_own(step, _):
-        rows = pl.ds(pl.multiple_of(8 * step, 8), 8)
-        start = pl.ds(pl.multiple_of(BINS * core + 8 * step, 8), 8)
-        got = swap_blocks([g_ref[k, start, :] for k in range(CHIPS)], 8)
-        for k1 in range(16):
-            h_ref[core, k1, rows, :] = got[k1]
-        return 0
-
-    def turn_other(step, _):
-        rows = pl.ds(pl.multiple_of(8 * step, 8), 8)
-        got = swap_blocks([o_ref[k, rows, :] for k in range(CHIPS)], 8)
-        for k1 in range(16):
-            h_ref[1 - core, k1, rows, :] = got[k1]
-        return 0
-
-    lax.fori_loop(0, WINDOW // 8, turn_own, 0)
+    part = WINDOW // 2
+
+    def turn_rows(read):
+        def body(step, _):
+            rows = pl.ds(pl.multiple_of(part * step, 8), part)
+            got = swap_blocks([read(k, part * step) for k in range(CHIPS)], 8)
+            for k1 in range(16):
+                h_ref[k1, rows, :] = got[k1]
+            return 0
+
+        lax.fori_loop(0, WINDOW // part, body, 0)
+
+    group = 4
+
+    def transform(from_core, add):
+        def body(step, _):
+            high, low = split(h_ref[pl.ds(group * step, group)].reshape(group * WINDOW, LANES))
+            d = jnp.dot(
+                jnp.concatenate([high, low, high], axis=1), az_fwd[from_core], preferred_element_type=F32
+            )
+            for k in range(group):
+                for c in range(2):
+                    piece = d[WINDOW * k : WINDOW * (k + 1), LANES * c : LANES * (c + 1)]
+                    if add:
+                        piece = piece + d_ref[group * step + k, c]
+                    d_ref[group * step + k, c] = piece
+            return 0
+
+        lax.fori_loop(0, 16 // group, body, 0)
+
+    turn_rows(lambda k, start: g_ref[k, pl.ds(pl.multiple_of(BINS * core + start, 8), part), :])
+    transform(core, False)
 
     def wait_core(row, _):
         core_copy(row).wait_recv()
         return 0
 
     lax.fori_loop(0, 4, wait_core, 0)
-    lax.fori_loop(0, WINDOW // 8, turn_other, 0)
-
-    def per_bin(k1, _):
-        d = times_right(jnp.concatenate([h_ref[0, k1], h_ref[1, k1]], axis=1), az_fwd[...])
+    turn_rows(lambda k, start: o_ref[k, pl.ds(pl.multiple_of(start, 8), part), :])
+    transform(1 - core, True)
+
+    def migrate(k1, slot):
         shift = shift_ref[pl.ds(k1, 1), :]
         weights = [w_ref[tap, pl.ds(k1, 1), :] for tap in range(TAPS)]
         moved = []
         for c in range(2):
-            x = d[:, LANES * c : LANES * (c + 1)]
+            x = d_ref[k1, c]
             near = jnp.where((shift & 16) != 0, x[16:80], x[0:64])
             x = jnp.concatenate([near, x[64:80]], axis=0)
-            d_ref[c, 0:72] = jnp.where((shift & 8) != 0, x[8:80], x[0:72])
-            e_ref[c, 0:64] = jnp.where((shift & 4) != 0, d_ref[c, 4:68], d_ref[c, 0:64])
-            d_ref[c, 0:62] = jnp.where((shift & 2) != 0, e_ref[c, 2:64], e_ref[c, 0:62])
-            e_ref[c, 0:61] = jnp.where((shift & 1) != 0, d_ref[c, 1:62], d_ref[c, 0:61])
-            total = weights[0] * e_ref[c, 5 : 5 + BINS]
+            m, e = m_ref.at[slot, c], e_ref.at[slot, c]
+            m[0:72] = jnp.where((shift & 8) != 0, x[8:80], x[0:72])
+            e[0:64] = jnp.where((shift & 4) != 0, m[4:68], m[0:64])
+            m[0:62] = jnp.where((shift & 2) != 0, e[2:64], e[0:62])
+            e[0:61] = jnp.where((shift & 1) != 0, m[1:62], m[0:61])
+            total = weights[0] * e[5 : 5 + BINS]
             for tap in range(1, TAPS):
-                total = total + weights[tap] * e_ref[c, 5 + tap : 5 + tap + BINS]
+                total = total + weights[tap] * e[5 + tap : 5 + tap + BINS]
             moved.append(total)
-        re, im = cmul(moved[0], moved[1], a_ref[0, k1], a_ref[1, k1])
-        s = times_right(jnp.concatenate([re, im], axis=1), az_back[...])
-        re, im = cmul(
-            s[:, :LANES], s[:, LANES:], az_twist[0, pl.ds(k1, 1), :], az_twist[1, pl.ds(k1, 1), :]
-        )
-        f_ref[0, k1] = re
-        f_ref[1, k1] = im
-        return 0
-
-    lax.fori_loop(0, 16, per_bin, 0)
+        return jnp.concatenate(cmul(moved[0], moved[1], a_ref[0, k1], a_ref[1, k1]), axis=1)
+
+    def per_group(step, _):
+        ks = [group * step + k for k in range(group)]
+        s = times_right(jnp.concatenate([migrate(k1, k) for k, k1 in enumerate(ks)], axis=0), az_back[...])
+        for k, k1 in enumerate(ks):
+            rows = slice(BINS * k, BINS * (k + 1))
+            f_ref[0, k1], f_ref[1, k1] = cmul(
+                s[rows, :LANES], s[rows, LANES:], az_twist[0, pl.ds(k1, 1), :], az_twist[1, pl.ds(k1, 1), :]
+            )
+        return 0
+
+    lax.fori_loop(0, 16 // group, per_group, 0)
 
     def finish(step, _):
         rows = pl.ds(pl.multiple_of(8 * step, 8), 8)
@@ -623,9 +674,10 @@
 
     lax.fori_loop(0, BINS // 8, finish, 0)
 
-    to_x.wait_send()
-    to_core(0).wait_send()
-    to_core(1).wait_send()
+    for r in range(LANE_PULSES):
+        for which in range(2):
+            x_copy(r, which).wait_send()
+            core_swap(r, which).wait_send()
 
     def wait_sends(t, _):
         def wait_z_send(off, _):
@@ -675,10 +727,13 @@
     loads[5 + 5] = like(tables[5], tables[5].shape[1:])
     scratch = [
         pltpu.VMEM((2, 2, 384, LANES), F32),
-        pltpu.VMEM((2, 2, LANE_PULSES, 48, LANES), F32),
-        pltpu.VMEM((2, LANE_PULSES, ROWS, LANES), F32),
+        pltpu.VMEM((LANE_PULSES, 2, 48, LANES), F32),
+        pltpu.VMEM((LANE_PULSES, 2, 48, LANES), F32),
+        pltpu.VMEM((LANE_PULSES, 2, 48, LANES), F32),
+        pltpu.VMEM((LANE_PULSES, 2, 48, LANES), F32),
+        pltpu.VMEM((LANE_PULSES, 2, ROWS, LANES), F32),
         pltpu.VMEM((2, ROWS, LANES), F32),
-        pltpu.VMEM((6 * ROWS, LANE_PULSES * LANES), BF16),
+        pltpu.VMEM((LANE_PULSES, 6 * ROWS, LANES), BF16),
         pltpu.VMEM((CHUNKS, PLANES, PIECE, LANES), F32),
         pltpu.VMEM((CHUNKS, PLANES * PIECE, LANES), F32),
         pltpu.VMEM((CHUNKS, CHUNK, LANES), F32),
@@ -687,11 +742,12 @@
         pltpu.VMEM((16, LANES), jnp.int32),
         pltpu.VMEM((TAPS, 16, LANES), F32),
         pltpu.VMEM((2, 16, BINS, LANES), F32),
-        pltpu.VMEM((2, 16, WINDOW, LANES), F32),
-        pltpu.VMEM((2, WINDOW, LANES), F32),
-        pltpu.VMEM((2, WINDOW, LANES), F32),
+        pltpu.VMEM((16, WINDOW, LANES), F32),
+        pltpu.VMEM((16, 2, WINDOW, LANES), F32),
+        pltpu.VMEM((4, 2, WINDOW, LANES), F32),
+        pltpu.VMEM((4, 2, WINDOW, LANES), F32),
         pltpu.VMEM((2, 16, BINS, LANES), F32),
-        DMA, DMA, DMA, DMA((2,)), DMA((2,)),
+        DMA((2,)), DMA((4, 2)), DMA((4, 2)), DMA((4, 2)), DMA((4, 2)),
         DMA((CHUNKS, PLANES)), DMA((CHUNKS, PLANES)), DMA((CHUNKS,)),
         DMA((CHUNKS, 4)), DMA((CHIPS,)), DMA((CHUNKS, 2)), DMA((CHIPS,)), DMA, DMA, DMA((4,)), DMA((4,)),
     ]

time: 94.2 us -> 81 us (0.86)
  Pallas kernels: 91.9 us -> 78.7 us
    pallas_call x1, Pallas kernels: 91.9 us -> 78.7 us  [shards(): pl.pallas_call(kernel, out_shape=jax.ShapeDtypeStruct((2, BINS, PULSES),...]
where the time goes in v2:
time: 81 us; the launch traced here: 80.7 us
  Pallas kernels  78.7 us (97%)
  local copies, waits for them, and re-layouts  2.06 us (3%)
    pallas_call x1, Pallas kernels, shards(): pl.pallas_call(kernel, out_shape=jax.ShapeDtypeStruct((2, BINS, PULSES),...  78.7 us
    unnamed x1, local copies, waits for them, and re-layouts  2.06 us

profile of v2, /device:TPU:1, one launch (start us, length us, event | category | flops | bytes accessed | tf_op | source)
XLA Modules:
  0.0 80.7 jit_solution(13328560001503655392)
XLA Ops:
  0.0 78.7 %shard_map.145 = f32[2,48,2048]{2,1,0:T(8,128)} custom-call(f32[2,2,384,128]{3,2,1,0:T(8,128)} %bitcast.13, f32[384,128]{1,0:T(8,128)} %bitcast.14, f32[2,48,2048]{2,1,0:T(8,128)} %azf_hbm.1, s32[16,128]{1,0:T(8,128)} %bitcast.15, s32[16,128]{1,0:T(8,128)} %bitcast.16, f32[8,16]{1,0:T(8,128)} %bitcast.17, bf16[384,1152]{1,0:T(8,128)(2,1)} %constant.18.clone.first_hbm, ...), custom_call_target="tpu_custom_call" | custom-call | tf_op jit(solution)/shard_map/pallas_call | solution.py:754
  78.7 2.1 %copy.18 = f32[2,48,2048]{2,1,0:T(8,128)} copy(f32[2,48,2048]{2,1,0:T(8,128)} %shard_map.145) | data formatting | bytes 1572864

commit v3 on v2

--- a/solution.py
+++ b/solution.py
@@ -32,7 +32,7 @@
 WINDOW = BELOW + BINS + ABOVE
 PAIR = BELOW + 2 * BINS + ABOVE
 TAPS = 8
-ORDER = (2, 1, 3, 0)
+ORDER = ((2, 1, 3, 0), (2, 3, 1, 0))
 
 
 def turn(product, period, sign):
@@ -304,11 +304,12 @@
             device_id_type=MESH,
         )
 
-    for r in range(LANE_PULSES):
+    def send_pulse(r):
         x_copy(r, 1).start()
         x_copy(r, 0).start()
-    for r in range(LANE_PULSES):
         core_swap(r, 0).start()
+
+    send_pulse(0)
 
     for load in loads:
         load.wait()
@@ -321,6 +322,7 @@
         x_copy(r, 1).wait_recv()
         core_swap(r, 1).start()
         x_copy(r, 0).wait_recv()
+        pl.when(r < LANE_PULSES - 1)(lambda: send_pulse(r + 1))
         core_swap(r, 0).wait_recv()
         core_swap(r, 1).wait_recv()
         twist_re, twist_im = twist[0], twist[1]
@@ -336,7 +338,8 @@
         v_ref[r, 4 * ROWS : 6 * ROWS] = high
 
     def chunk_of(t):
-        step = jnp.where(t == 0, ORDER[0], jnp.where(t == 1, ORDER[1], jnp.where(t == 2, ORDER[2], ORDER[3])))
+        one, three = jnp.where(core == 0, t == 1, t == 2), jnp.where(core == 0, t == 2, t == 1)
+        step = jnp.where(t == 0, 2, jnp.where(one, 1, jnp.where(three, 3, 0)))
         return lax.rem(y + step, CHUNKS)
 
     def z_copy(block, off):
@@ -356,7 +359,8 @@
         )
 
     def send_block(block):
-        def start(near, _):
+        def start(step, _):
+            near = PLANES // 2 - step
             z_copy(block, near).start()
             z_copy(block, PLANES - near).start()
             return 0
@@ -364,6 +368,13 @@
         z_copy(block, PLANES // 2).start()
         lax.fori_loop(1, PLANES // 2, start, 0)
         z_mine(block).start()
+
+    def sent_block(block):
+        def wait_z_send(off, _):
+            z_copy(block, off).wait_send()
+            return 0
+
+        lax.fori_loop(1, PLANES, wait_z_send, 0)
 
     size = 2 * CHUNK_ROWS
 
@@ -386,7 +397,6 @@
                     y_ref[2 + pair, to, place : place + size, :] = out[
                         size * to : size * (to + 1), LANES * r : LANES * (r + 1)
                     ]
-        send_block(2 + pair)
         return 0
 
     def later_pulse(r, _):
@@ -418,6 +428,13 @@
         for row in range(16):
             weight = jnp.where(frac == row, ktab[tap, row], weight)
         w_ref[tap] = weight
+
+    def next_block(block, _):
+        sent_block(block)
+        send_block(block + 2)
+        return 0
+
+    lax.fori_loop(0, 2, next_block, 0)
 
     def main_copy(t, q, src, dst, size):
         return pltpu.make_async_remote_copy(
@@ -680,11 +697,7 @@
             core_swap(r, which).wait_send()
 
     def wait_sends(t, _):
-        def wait_z_send(off, _):
-            z_copy(t, off).wait_send()
-            return 0
-
-        lax.fori_loop(1, PLANES, wait_z_send, 0)
+        pl.when(t >= 2)(lambda: sent_block(t))
         each_main(t, lambda *a: main_copy(*a).wait_send())
         each_halo(t, lambda *a: halo_copy(*a).wait_send(), lambda *a: None)
         core_copy(t).wait_send()

time: 81 us -> 79.4 us (0.980)
  Pallas kernels: 78.7 us -> 77.2 us
    pallas_call x1, Pallas kernels: 78.7 us -> 77.2 us  [shards(): pl.pallas_call(kernel, out_shape=jax.ShapeDtypeStruct((2, BINS, PULSES),...]
where the time goes in v3:
time: 79.4 us; the launch traced here: 79.3 us
  Pallas kernels  77.2 us (97%)
  local copies, waits for them, and re-layouts  2.06 us (3%)
    pallas_call x1, Pallas kernels, shards(): pl.pallas_call(kernel, out_shape=jax.ShapeDtypeStruct((2, BINS, PULSES),...  77.2 us
    unnamed x1, local copies, waits for them, and re-layouts  2.06 us

profile of v3, /device:TPU:1, one launch (start us, length us, event | category | flops | bytes accessed | tf_op | source)
XLA Modules:
  0.0 79.3 jit_solution(13676682352607440671)
XLA Ops:
  0.0 77.2 %shard_map.145 = f32[2,48,2048]{2,1,0:T(8,128)} custom-call(f32[2,2,384,128]{3,2,1,0:T(8,128)} %bitcast.13, f32[384,128]{1,0:T(8,128)} %bitcast.14, f32[2,48,2048]{2,1,0:T(8,128)} %azf_hbm.1, s32[16,128]{1,0:T(8,128)} %bitcast.15, s32[16,128]{1,0:T(8,128)} %bitcast.16, f32[8,16]{1,0:T(8,128)} %bitcast.17, bf16[384,1152]{1,0:T(8,128)(2,1)} %constant.18.clone.first_hbm, ...), custom_call_target="tpu_custom_call" | custom-call | tf_op jit(solution)/shard_map/pallas_call | solution.py:767
  77.2 2.1 %copy.18 = f32[2,48,2048]{2,1,0:T(8,128)} copy(f32[2,48,2048]{2,1,0:T(8,128)} %shard_map.145) | data formatting | bytes 1572864

commit v4 on v3

--- a/solution.py
+++ b/solution.py
@@ -184,13 +184,13 @@
 def kernel(
     raw_hbm, filt_hbm, azf_hbm, shift_hbm, frac_hbm, ktab_hbm,
     first_hbm, last_hbm, twist_hbm, fwd_hbm, back_hbm, planes_hbm, az_fwd_hbm, az_back_hbm, az_twist_hbm,
-    out_ref,
+    out_hbm,
     filt_in, azf_in, shift_in, frac_in, ktab, first, last, twist, fwd, back, planes, az_fwd, az_back, az_twist,
     load_sem,
     tiles, to_like, to_relay, relay, to_core, x_ref, filt, v_ref, y_ref, z_ref, t_ref, g_ref, o_ref,
     shift_ref, w_ref, a_ref, h_ref, d_ref, m_ref, e_ref, f_ref,
-    tile_sem, x_send, x_recv, core_send, core_recv, z_send, z_recv, z_own,
-    p_send, p_recv, h_send, h_recv, own_sem, halo_own, fwd_send, fwd_recv,
+    tile_sem, x_send, x_recv, core_send, core_recv, z_send, z_recv,
+    p_send, p_recv, h_send, h_recv, fwd_send, fwd_recv, out_sem,
 ):
     pulse = lax.axis_index("pulse")
     lane = lax.axis_index("rng")
@@ -208,34 +208,6 @@
 
     x_partner = (pulse, 2 * (1 - xh) + core)
     core_partner = (pulse, 2 * xh + 1 - core)
-
-    barrier = pltpu.get_barrier_semaphore()
-
-    def greet(to):
-        pl.semaphore_signal(barrier, inc=1, device_id=to, device_id_type=MESH)
-
-    greet(x_partner)
-    greet(core_partner)
-
-    def greet_z(off, _):
-        greet(device(lax.rem(z + off, PLANES), chip, core))
-        return 0
-
-    def greet_plane(off, _):
-        greet(device(z, lax.rem(chip + off, CHIPS), core))
-        return 0
-
-    def greet_all(plane):
-        def body(other, _):
-            greet(device(plane, other, core))
-            return 0
-
-        lax.fori_loop(0, CHIPS, body, 0)
-
-    lax.fori_loop(1, PLANES, greet_z, 0)
-    lax.fori_loop(1, CHIPS, greet_plane, 0)
-    pl.when(jnp.logical_and(chip == 0, has_below))(lambda: greet_all(z - 1))
-    pl.when(jnp.logical_and(chip == CHIPS - 1, has_above))(lambda: greet_all(z + 1))
 
     place = 2 * chip + core
     loads = [
@@ -249,7 +221,38 @@
         pltpu.make_async_copy(raw_hbm.at[:, 1 - xh], tiles.at[1], tile_sem.at[1]),
         pltpu.make_async_copy(raw_hbm.at[:, xh], tiles.at[0], tile_sem.at[0]),
     ]
-    for load in tile_loads + loads:
+    for load in tile_loads:
+        load.start()
+
+    barrier = pltpu.get_barrier_semaphore()
+
+    def greet(to):
+        pl.semaphore_signal(barrier, inc=1, device_id=to, device_id_type=MESH)
+
+    greet(x_partner)
+    greet(core_partner)
+
+    def greet_z(off, _):
+        greet(device(lax.rem(z + off, PLANES), chip, core))
+        return 0
+
+    def greet_plane(off, _):
+        greet(device(z, lax.rem(chip + off, CHIPS), core))
+        return 0
+
+    def greet_all(plane):
+        def body(other, _):
+            greet(device(plane, other, core))
+            return 0
+
+        lax.fori_loop(0, CHIPS, body, 0)
+
+    lax.fori_loop(1, PLANES, greet_z, 0)
+    lax.fori_loop(1, CHIPS, greet_plane, 0)
+    pl.when(jnp.logical_and(chip == 0, has_below))(lambda: greet_all(z - 1))
+    pl.when(jnp.logical_and(chip == CHIPS - 1, has_above))(lambda: greet_all(z + 1))
+
+    for load in loads:
         load.start()
 
     def blank(start, size):
@@ -270,7 +273,7 @@
 
     for load in tile_loads:
         load.wait()
-    for r in range(LANE_PULSES):
+    def sort_pulse(r):
         like = pl.ds(4 * core + r, 48, stride=8)
         other = pl.ds(4 * (1 - core) + r, 48, stride=8)
         for c in range(2):
@@ -279,6 +282,7 @@
             to_core[r, c] = tiles[0, c, other, :]
             x_ref[r, c, quarter_rows(my_quarter), :] = tiles[0, c, like, :]
 
+    sort_pulse(0)
     pl.semaphore_wait(
         barrier,
         2 + PLANES - 1 + CHIPS - 1 + jnp.where(has_below, 1, 0) + jnp.where(has_above, 1, 0),
@@ -310,6 +314,8 @@
         core_swap(r, 0).start()
 
     send_pulse(0)
+    for r in range(1, LANE_PULSES):
+        sort_pulse(r)
 
     for load in loads:
         load.wait()
@@ -347,15 +353,15 @@
         return pltpu.make_async_remote_copy(
             src_ref=y_ref.at[block, to],
             dst_ref=z_ref.at[block, pl.ds(pl.multiple_of(PIECE * z, 8), PIECE)],
-            send_sem=z_send.at[block, off],
-            recv_sem=z_recv.at[block, off],
+            send_sem=z_send.at[block],
+            recv_sem=z_recv.at[block],
             device_id=device(to, chip, core),
             device_id_type=MESH,
         )
 
     def z_mine(block):
         return pltpu.make_async_copy(
-            y_ref.at[block, z], z_ref.at[block, pl.ds(pl.multiple_of(PIECE * z, 8), PIECE)], z_own.at[block]
+            y_ref.at[block, z], z_ref.at[block, pl.ds(pl.multiple_of(PIECE * z, 8), PIECE)], z_recv.at[block]
         )
 
     def send_block(block):
@@ -369,12 +375,11 @@
         lax.fori_loop(1, PLANES // 2, start, 0)
         z_mine(block).start()
 
+    def wait_for(ref, sem):
+        pltpu.make_async_copy(ref, ref, sem).wait()
+
     def sent_block(block):
-        def wait_z_send(off, _):
-            z_copy(block, off).wait_send()
-            return 0
-
-        lax.fori_loop(1, PLANES, wait_z_send, 0)
+        wait_for(y_ref.at[block, pl.ds(0, PLANES - 1)], z_send.at[block])
 
     size = 2 * CHUNK_ROWS
 
@@ -429,6 +434,11 @@
             weight = jnp.where(frac == row, ktab[tap, row], weight)
         w_ref[tap] = weight
 
+    for r in range(LANE_PULSES):
+        for which in range(2):
+            x_copy(r, which).wait_send()
+            core_swap(r, which).wait_send()
+
     def next_block(block, _):
         sent_block(block)
         send_block(block + 2)
@@ -441,24 +451,14 @@
             src_ref=t_ref.at[t, pl.ds(src, size)],
             dst_ref=g_ref.at[chip, pl.ds(dst, size)],
             send_sem=p_send.at[t, q],
-            recv_sem=p_recv.at[chip],
+            recv_sem=p_recv.at[y],
             device_id=device(z, 4 * chunk_of(t) + q, core),
             device_id_type=MESH,
         )
 
-    def main_recv(other, src, dst, size):
-        return pltpu.make_async_remote_copy(
-            src_ref=t_ref.at[0, pl.ds(src, size)],
-            dst_ref=g_ref.at[other, pl.ds(dst, size)],
-            send_sem=p_send.at[0, 0],
-            recv_sem=p_recv.at[other],
-            device_id=core_partner,
-            device_id_type=MESH,
-        )
-
     def main_own(src, dst, size):
         return pltpu.make_async_copy(
-            t_ref.at[CHUNKS - 1, pl.ds(src, size)], g_ref.at[chip, pl.ds(dst, size)], own_sem
+            t_ref.at[CHUNKS - 1, pl.ds(src, size)], g_ref.at[chip, pl.ds(dst, size)], p_recv.at[y]
         )
 
     def windows(q, act):
@@ -483,7 +483,7 @@
             src_ref=t_ref.at[t, pl.ds(src, size)],
             dst_ref=g_ref.at[chip, pl.ds(dst, size)],
             send_sem=h_send.at[t, which],
-            recv_sem=h_recv.at[chip],
+            recv_sem=h_recv.at[y],
             device_id=device(plane, to, core),
             device_id_type=MESH,
         )
@@ -491,18 +491,7 @@
     def halo_mine(t, which):
         src, dst, size = (DOWN, UP)[which]
         return pltpu.make_async_copy(
-            t_ref.at[t, pl.ds(src, size)], g_ref.at[chip, pl.ds(dst, size)], halo_own
-        )
-
-    def halo_recv(other, which):
-        src, dst, size = (DOWN, UP)[which]
-        return pltpu.make_async_remote_copy(
-            src_ref=t_ref.at[0, pl.ds(src, size)],
-            dst_ref=g_ref.at[other, pl.ds(dst, size)],
-            send_sem=h_send.at[0, which],
-            recv_sem=h_recv.at[other],
-            device_id=core_partner,
-            device_id_type=MESH,
+            t_ref.at[t, pl.ds(src, size)], g_ref.at[chip, pl.ds(dst, size)], h_recv.at[y]
         )
 
     def each_halo(t, remote, local):
@@ -526,12 +515,12 @@
             pl.when(jnp.logical_not(to_me))(remote)
 
     def wait_block(block, _):
-        def wait_z(off, _):
-            z_copy(block, off).wait_recv()
-            return 0
-
-        lax.fori_loop(1, PLANES, wait_z, 0)
-        z_mine(block).wait()
+        wait_for(z_ref.at[block], z_recv.at[block])
+        return 0
+
+    def sent_chunk(t, _):
+        each_main(t, lambda *a: main_copy(*a).wait_send())
+        each_halo(t, lambda *a: halo_copy(*a).wait_send(), lambda *a: None)
         return 0
 
     def plane_step(t, _):
@@ -541,6 +530,7 @@
 
         @pl.when(t == 2)
         def _():
+            lax.fori_loop(0, 2, sent_chunk, 0)
             wait_block(3, 0)
 
         pair = lax.div(t, 2)
@@ -560,20 +550,12 @@
             )
         each_main(t, lambda *a: main_copy(*a).start())
 
-        def local(t, which):
-            halo_mine(t, which).start()
-            halo_mine(t, which).wait()
-
-        each_halo(t, lambda *a: halo_copy(*a).start(), local)
+        each_halo(t, lambda *a: halo_copy(*a).start(), lambda *a: halo_mine(*a).start())
         return 0
 
     lax.fori_loop(0, CHUNKS, plane_step, 0)
 
-    def own(src, dst, size):
-        main_own(src, dst, size).start()
-        main_own(src, dst, size).wait()
-
-    windows(q_me, own)
+    windows(q_me, lambda *a: main_own(*a).start())
 
     def core_copy(row):
         return pltpu.make_async_remote_copy(
@@ -587,23 +569,16 @@
 
     takes_up = jnp.logical_and(q_me == 0, jnp.logical_or(y > 0, has_below))
     takes_down = jnp.logical_and(q_me == 3, jnp.logical_or(y < 3, has_above))
-    other_plane = jnp.where(q_me == 0, y == 0, y == 3)
 
     def gather(t, _):
         row = lax.rem(y + CHUNKS - chunk_of(t) + y, CHUNKS)
 
-        def one(k, _):
-            other = 4 * row + k
-            mine = other == chip
-            pl.when(jnp.logical_not(mine))(
-                lambda: windows(q_me, lambda *a: main_recv(other, *a).wait_recv())
-            )
-            remote = jnp.logical_or(other_plane, jnp.logical_not(mine))
-            pl.when(jnp.logical_and(takes_up, remote))(lambda: halo_recv(other, 1).wait_recv())
-            pl.when(jnp.logical_and(takes_down, remote))(lambda: halo_recv(other, 0).wait_recv())
-            return 0
-
-        lax.fori_loop(0, 4, one, 0)
+        def rows_of(start, size):
+            return g_ref.at[pl.ds(4 * row, 4), pl.ds(start, size)]
+
+        windows(q_me, lambda src, dst, size: wait_for(rows_of(dst, size), p_recv.at[row]))
+        pl.when(takes_up)(lambda: wait_for(rows_of(0, BELOW), h_recv.at[row]))
+        pl.when(takes_down)(lambda: wait_for(rows_of(PAIR - ABOVE, ABOVE), h_recv.at[row]))
         core_copy(row).start()
         return 0
 
@@ -646,6 +621,9 @@
         core_copy(row).wait_recv()
         return 0
 
+    lax.fori_loop(2, 4, sent_chunk, 0)
+    for block in (2, 3):
+        sent_block(block)
     lax.fori_loop(0, 4, wait_core, 0)
     turn_rows(lambda k, start: o_ref[k, pl.ds(pl.multiple_of(start, 8), part), :])
     transform(1 - core, True)
@@ -669,6 +647,10 @@
             moved.append(total)
         return jnp.concatenate(cmul(moved[0], moved[1], a_ref[0, k1], a_ref[1, k1]), axis=1)
 
+    def result_copy(step):
+        some = pl.ds(group * step, group)
+        return pltpu.make_async_copy(f_ref.at[:, some], out_hbm.at[:, some], out_sem.at[step])
+
     def per_group(step, _):
         ks = [group * step + k for k in range(group)]
         s = times_right(jnp.concatenate([migrate(k1, k) for k, k1 in enumerate(ks)], axis=0), az_back[...])
@@ -677,33 +659,30 @@
             f_ref[0, k1], f_ref[1, k1] = cmul(
                 s[rows, :LANES], s[rows, LANES:], az_twist[0, pl.ds(k1, 1), :], az_twist[1, pl.ds(k1, 1), :]
             )
+        result_copy(step).start()
         return 0
 
     lax.fori_loop(0, 16 // group, per_group, 0)
 
-    def finish(step, _):
-        rows = pl.ds(pl.multiple_of(8 * step, 8), 8)
+    def sent_core(row, _):
+        core_copy(row).wait_send()
+        return 0
+
+    lax.fori_loop(0, 4, sent_core, 0)
+    for step in range(16 // group):
+        result_copy(step).wait()
+
+
+FINISH_ROWS = 16
+
+
+def finish_kernel(f_ref, out_ref):
+    for half in range(FINISH_ROWS // 8):
+        rows = slice(8 * half, 8 * (half + 1))
         got = fft_list([(f_ref[0, k1, rows, :], f_ref[1, k1, rows, :]) for k1 in range(16)], 1)
         for tile in range(16):
-            out_ref[0, rows, LANES * tile : LANES * (tile + 1)] = got[tile][0]
-            out_ref[1, rows, LANES * tile : LANES * (tile + 1)] = got[tile][1]
-        return 0
-
-    lax.fori_loop(0, BINS // 8, finish, 0)
-
-    for r in range(LANE_PULSES):
-        for which in range(2):
-            x_copy(r, which).wait_send()
-            core_swap(r, which).wait_send()
-
-    def wait_sends(t, _):
-        pl.when(t >= 2)(lambda: sent_block(t))
-        each_main(t, lambda *a: main_copy(*a).wait_send())
-        each_halo(t, lambda *a: halo_copy(*a).wait_send(), lambda *a: None)
-        core_copy(t).wait_send()
-        return 0
-
-    lax.fori_loop(0, CHUNKS, wait_sends, 0)
+            for c in range(2):
+                out_ref[c, rows, LANES * tile : LANES * (tile + 1)] = got[tile][c]
 
 
 ANY = pl.BlockSpec(memory_space=pl.ANY)
@@ -761,19 +740,26 @@
         pltpu.VMEM((4, 2, WINDOW, LANES), F32),
         pltpu.VMEM((2, 16, BINS, LANES), F32),
         DMA((2,)), DMA((4, 2)), DMA((4, 2)), DMA((4, 2)), DMA((4, 2)),
-        DMA((CHUNKS, PLANES)), DMA((CHUNKS, PLANES)), DMA((CHUNKS,)),
-        DMA((CHUNKS, 4)), DMA((CHIPS,)), DMA((CHUNKS, 2)), DMA((CHIPS,)), DMA, DMA, DMA((4,)), DMA((4,)),
+        DMA((4,)), DMA((4,)),
+        DMA((CHUNKS, 4)), DMA((4,)), DMA((CHUNKS, 2)), DMA((4,)), DMA((4,)), DMA((4,)), DMA((4,)),
     ]
-    return pl.pallas_call(
+    turned = pl.pallas_call(
         kernel,
-        out_shape=jax.ShapeDtypeStruct((2, BINS, PULSES), F32),
+        out_shape=jax.ShapeDtypeStruct((2, 16, BINS, LANES), F32),
         in_specs=[ANY] * (len(operands) + len(tables)),
-        out_specs=pl.BlockSpec(memory_space=pltpu.VMEM),
+        out_specs=ANY,
         scratch_shapes=loads + [DMA((len(loads),))] + scratch,
         compiler_params=pltpu.CompilerParams(
             vmem_limit_bytes=60 * 2**20, collective_id=0, has_side_effects=True
         ),
     )(*operands, *tables)
+    return pl.pallas_call(
+        finish_kernel,
+        out_shape=jax.ShapeDtypeStruct((2, BINS, PULSES), F32),
+        grid=(BINS // FINISH_ROWS,),
+        in_specs=[pl.BlockSpec((2, 16, FINISH_ROWS, LANES), lambda i: (0, 0, i, 0))],
+        out_specs=pl.BlockSpec((2, FINISH_ROWS, PULSES), lambda i: (0, i, 0)),
+    )(turned)
 
 
 def solution(mesh):

time: 79.4 us -> 78.9 us (level); the launches traced: 79.3 us -> 77.6 us
  local copies, waits for them, and re-layouts: 2.06 us -> 0 us
    unnamed x1 -> x0, local copies, waits for them, and re-layouts: 2.06 us -> none
    pallas_call x1 -> x2, Pallas kernels: 77.2 us -> 77.6 us  [the longest x1 74.6 us: shards(): pl.pallas_call(kernel, out_shape=jax.ShapeDtypeStruct((2, 16, BINS, LANES...]
where the time goes in v4:
time: 78.9 us; the launch traced here: 77.6 us
  Pallas kernels  77.6 us (98%)
    pallas_call x1, Pallas kernels, shards(): pl.pallas_call(kernel, out_shape=jax.ShapeDtypeStruct((2, 16, BINS, LANES...  74.6 us
    pallas_call x1, Pallas kernels, shards(): pl.pallas_call(finish_kernel, out_shape=jax.ShapeDtypeStruct((2, BINS, PU...  2.95 us

profile of v4, /device:TPU:1, one launch (start us, length us, event | category | flops | bytes accessed | tf_op | source)
XLA Modules:
  0.0 77.6 jit_solution(14643260411959656417)
XLA Ops:
  0.0 74.6 %shard_map.145.f_ref = f32[2,16,48,128]{3,2,1,0:T(8,128)} custom-call(f32[2,2,384,128]{3,2,1,0:T(8,128)} %bitcast.13, f32[384,128]{1,0:T(8,128)} %bitcast.14, f32[2,48,2048]{2,1,0:T(8,128)} %azf_hbm.1, s32[16,128]{1,0:T(8,128)} %bitcast.15, s32[16,128]{1,0:T(8,128)} %bitcast.16, f32[8,16]{1,0:T(8,128)} %bitcast.17, ...), custom_call_target="tpu_custom_call" | custom-call | tf_op jit(solution)/shard_map/pallas_call | solution.py:746
  74.6 2.9 %shard_map.146 = f32[2,48,2048]{2,1,0:T(8,128)} custom-call(f32[2,16,48,128]{3,2,1,0:T(8,128)} %shard_map.145.f_ref), custom_call_target="tpu_custom_call" | custom-call | tf_op jit(solution)/shard_map/pallas_call | solution.py:756

commit v5 on v4

--- a/solution.py
+++ b/solution.py
@@ -26,12 +26,13 @@
 CHUNKS = 4
 CHUNK_ROWS = 3
 CHUNK = CHUNK_ROWS * LANES
-PIECE = 2 * CHUNK_ROWS * LANE_PULSES
+BLOCKS = (24, 24, 32, 16)
 BELOW = 8
 ABOVE = 24
 WINDOW = BELOW + BINS + ABOVE
 PAIR = BELOW + 2 * BINS + ABOVE
 TAPS = 8
+NEAR = 4
 ORDER = ((2, 1, 3, 0), (2, 3, 1, 0))
 
 
@@ -187,9 +188,9 @@
     out_hbm,
     filt_in, azf_in, shift_in, frac_in, ktab, first, last, twist, fwd, back, planes, az_fwd, az_back, az_twist,
     load_sem,
-    tiles, to_like, to_relay, relay, to_core, x_ref, filt, v_ref, y_ref, z_ref, t_ref, g_ref, o_ref,
+    tiles, to_like, to_cross, to_core, x_ref, filt, v_ref, y0, y1, y2, y3, z0, z1, z2, z3, t_ref, g_ref, o_ref,
     shift_ref, w_ref, a_ref, h_ref, d_ref, m_ref, e_ref, f_ref,
-    tile_sem, x_send, x_recv, core_send, core_recv, z_send, z_recv,
+    tile_sem, x_send, x_recv, z_send, z_recv,
     p_send, p_recv, h_send, h_recv, fwd_send, fwd_recv, out_sem,
 ):
     pulse = lax.axis_index("pulse")
@@ -207,6 +208,7 @@
         return (8 * plane + lax.div(other_chip, 2), 2 * lax.rem(other_chip, 2) + other_core)
 
     x_partner = (pulse, 2 * (1 - xh) + core)
+    x_cross = (pulse, 2 * (1 - xh) + 1 - core)
     core_partner = (pulse, 2 * xh + 1 - core)
 
     place = 2 * chip + core
@@ -230,6 +232,7 @@
         pl.semaphore_signal(barrier, inc=1, device_id=to, device_id_type=MESH)
 
     greet(x_partner)
+    greet(x_cross)
     greet(core_partner)
 
     def greet_z(off, _):
@@ -266,7 +269,6 @@
     pl.when(jnp.logical_and(chip == CHIPS - 1, z == PLANES - 1))(lambda: blank(PAIR - ABOVE, ABOVE))
 
     my_quarter = 2 * xh + core
-    x_quarter = 2 * (1 - xh) + core
 
     def quarter_rows(quarter):
         return pl.ds(pl.multiple_of(48 * quarter, 8), 48)
@@ -278,40 +280,29 @@
         other = pl.ds(4 * (1 - core) + r, 48, stride=8)
         for c in range(2):
             to_like[r, c] = tiles[1, c, like, :]
-            to_relay[r, c] = tiles[1, c, other, :]
+            to_cross[r, c] = tiles[1, c, other, :]
             to_core[r, c] = tiles[0, c, other, :]
             x_ref[r, c, quarter_rows(my_quarter), :] = tiles[0, c, like, :]
 
     sort_pulse(0)
     pl.semaphore_wait(
         barrier,
-        2 + PLANES - 1 + CHIPS - 1 + jnp.where(has_below, 1, 0) + jnp.where(has_above, 1, 0),
+        3 + PLANES - 1 + CHIPS - 1 + jnp.where(has_below, 1, 0) + jnp.where(has_above, 1, 0),
     )
 
-    def x_copy(r, which):
+    def pulse_copy(r, which):
         return pltpu.make_async_remote_copy(
-            src_ref=(to_like, to_relay)[which].at[r],
-            dst_ref=x_ref.at[r, :, quarter_rows(my_quarter)] if which == 0 else relay.at[r],
+            src_ref=(to_like, to_cross, to_core)[which].at[r],
+            dst_ref=x_ref.at[r, :, quarter_rows(my_quarter)],
             send_sem=x_send.at[r, which],
             recv_sem=x_recv.at[r, which],
-            device_id=x_partner,
+            device_id=(x_partner, x_cross, core_partner)[which],
             device_id_type=MESH,
         )
 
-    def core_swap(r, which):
-        return pltpu.make_async_remote_copy(
-            src_ref=(to_core, relay)[which].at[r],
-            dst_ref=x_ref.at[r, :, quarter_rows((my_quarter, x_quarter)[which])],
-            send_sem=core_send.at[r, which],
-            recv_sem=core_recv.at[r, which],
-            device_id=core_partner,
-            device_id_type=MESH,
-        )
-
     def send_pulse(r):
-        x_copy(r, 1).start()
-        x_copy(r, 0).start()
-        core_swap(r, 0).start()
+        for which in range(3):
+            pulse_copy(r, which).start()
 
     send_pulse(0)
     for r in range(1, LANE_PULSES):
@@ -325,12 +316,9 @@
         filt[c] = jnp.concatenate([tall[:ROWS], tall[ROWS:]], axis=1)
 
     def compress(r):
-        x_copy(r, 1).wait_recv()
-        core_swap(r, 1).start()
-        x_copy(r, 0).wait_recv()
+        for which in range(3):
+            pulse_copy(r, which).wait_recv()
         pl.when(r < LANE_PULSES - 1)(lambda: send_pulse(r + 1))
-        core_swap(r, 0).wait_recv()
-        core_swap(r, 1).wait_recv()
         twist_re, twist_im = twist[0], twist[1]
         v = times_left(first[...], jnp.concatenate([x_ref[r, 0], x_ref[r, 1]], axis=0))
         re, im = cmul(v[:ROWS], v[ROWS:], twist_re, twist_im)
@@ -343,16 +331,21 @@
         v_ref[r, 2 * ROWS : 4 * ROWS] = low
         v_ref[r, 4 * ROWS : 6 * ROWS] = high
 
+    ys, zs = (y0, y1, y2, y3), (z0, z1, z2, z3)
+
     def chunk_of(t):
-        one, three = jnp.where(core == 0, t == 1, t == 2), jnp.where(core == 0, t == 2, t == 1)
-        step = jnp.where(t == 0, 2, jnp.where(one, 1, jnp.where(three, 3, 0)))
-        return lax.rem(y + step, CHUNKS)
+        if t in (0, 3):
+            return lax.rem(y + (2 if t == 0 else 0), CHUNKS)
+        return lax.rem(y + jnp.where(core == t - 1, 1, 3), CHUNKS)
+
+    def z_mine_rows(block):
+        return pl.ds(pl.multiple_of(BLOCKS[block] * z, 8), BLOCKS[block])
 
     def z_copy(block, off):
         to = lax.rem(z + off, PLANES)
         return pltpu.make_async_remote_copy(
-            src_ref=y_ref.at[block, to],
-            dst_ref=z_ref.at[block, pl.ds(pl.multiple_of(PIECE * z, 8), PIECE)],
+            src_ref=ys[block].at[to],
+            dst_ref=zs[block].at[z_mine_rows(block)],
             send_sem=z_send.at[block],
             recv_sem=z_recv.at[block],
             device_id=device(to, chip, core),
@@ -360,57 +353,71 @@
         )
 
     def z_mine(block):
-        return pltpu.make_async_copy(
-            y_ref.at[block, z], z_ref.at[block, pl.ds(pl.multiple_of(PIECE * z, 8), PIECE)], z_recv.at[block]
-        )
-
-    def send_block(block):
+        return pltpu.make_async_copy(ys[block].at[z], zs[block].at[z_mine_rows(block)], z_recv.at[block])
+
+    def send_to(block, first, last):
         def start(step, _):
-            near = PLANES // 2 - step
+            near = last - step
             z_copy(block, near).start()
             z_copy(block, PLANES - near).start()
             return 0
 
+        lax.fori_loop(0, last - first + 1, start, 0)
+
+    def send_far(block):
         z_copy(block, PLANES // 2).start()
-        lax.fori_loop(1, PLANES // 2, start, 0)
+        send_to(block, NEAR + 1, PLANES // 2 - 1)
         z_mine(block).start()
+
+    def send_near(block):
+        send_to(block, 1, NEAR)
+
+    def send_block(block):
+        send_far(block)
+        send_near(block)
 
     def wait_for(ref, sem):
         pltpu.make_async_copy(ref, ref, sem).wait()
 
     def sent_block(block):
-        wait_for(y_ref.at[block, pl.ds(0, PLANES - 1)], z_send.at[block])
+        wait_for(ys[block].at[pl.ds(0, PLANES - 1)], z_send.at[block])
 
     size = 2 * CHUNK_ROWS
 
-    def one_pulse(r, _):
+    def place_of(t, r, c, row):
+        if t == 3:
+            return 3, 6 * (r - 2) + 3 * c + row
+        if t < 2:
+            return 2, 12 * t + 6 * (r - 2) + 3 * c + row
+        if row < 2:
+            return 2, 24 + 4 * (r - 2) + 2 * c + row
+        return 3, 12 + 2 * (r - 2) + c
+
+    for r in range(2):
         compress(r)
         for chunk in range(CHUNKS):
             out = jnp.dot(last[chunk], v_ref[r], preferred_element_type=F32)
             for to in range(PLANES):
-                y_ref[r, to, size * chunk : size * (chunk + 1), :] = out[size * to : size * (to + 1)]
+                ys[r][to, size * chunk : size * (chunk + 1), :] = out[size * to : size * (to + 1)]
         send_block(r)
-        return 0
-
-    def two_chunks(pair, _):
-        both = jnp.concatenate([v_ref[2], v_ref[3]], axis=1)
-        for half in range(2):
-            out = jnp.dot(last[chunk_of(2 * pair + half)], both, preferred_element_type=F32)
-            for r in range(2):
-                place = size * (2 * half + r)
-                for to in range(PLANES):
-                    y_ref[2 + pair, to, place : place + size, :] = out[
-                        size * to : size * (to + 1), LANES * r : LANES * (r + 1)
-                    ]
-        return 0
 
     def later_pulse(r, _):
         compress(r)
         return 0
 
-    lax.fori_loop(0, 2, one_pulse, 0)
     lax.fori_loop(2, 4, later_pulse, 0)
-    lax.fori_loop(0, 2, two_chunks, 0)
+    both = jnp.concatenate([v_ref[2], v_ref[3]], axis=1)
+    for t in range(CHUNKS):
+        out = jnp.dot(last[chunk_of(t)], both, preferred_element_type=F32)
+        for r in (2, 3):
+            lanes = slice(LANES * (r - 2), LANES * (r - 1))
+            pieces = [(0, 6)] if t != 2 else [(0, 2), (2, 3), (3, 5), (5, 6)]
+            for first_row, end in pieces:
+                block, place = place_of(t, r, first_row // 3, first_row % 3)
+                for to in range(PLANES):
+                    ys[block][to, place : place + end - first_row, :] = out[
+                        size * to + first_row : size * to + end, lanes
+                    ]
 
     def turn_filter(step, _):
         rows = pl.ds(pl.multiple_of(8 * step, 8), 8)
@@ -435,18 +442,25 @@
         w_ref[tap] = weight
 
     for r in range(LANE_PULSES):
-        for which in range(2):
-            x_copy(r, which).wait_send()
-            core_swap(r, which).wait_send()
-
-    def next_block(block, _):
-        sent_block(block)
-        send_block(block + 2)
-        return 0
-
-    lax.fori_loop(0, 2, next_block, 0)
-
-    def main_copy(t, q, src, dst, size):
+        for which in range(3):
+            pulse_copy(r, which).wait_send()
+
+    sent_block(0)
+    send_block(2)
+    sent_block(1)
+    send_far(3)
+    sent_block(2)
+    send_near(3)
+
+    def window(q):
+        if q == 0:
+            return 0, BELOW, PAIR - BELOW
+        if q == 3:
+            return CHUNK - BELOW - 2 * BINS, 0, PAIR - ABOVE
+        return 2 * BINS * q - BELOW, 0, PAIR
+
+    def main_copy(t, q):
+        src, dst, size = window(q)
         return pltpu.make_async_remote_copy(
             src_ref=t_ref.at[t, pl.ds(src, size)],
             dst_ref=g_ref.at[chip, pl.ds(dst, size)],
@@ -456,16 +470,24 @@
             device_id_type=MESH,
         )
 
-    def main_own(src, dst, size):
+    def main_own(q):
+        src, dst, size = window(q)
         return pltpu.make_async_copy(
             t_ref.at[CHUNKS - 1, pl.ds(src, size)], g_ref.at[chip, pl.ds(dst, size)], p_recv.at[y]
         )
 
-    def windows(q, act):
-        pl.when(q == 0)(lambda: act(0, BELOW, PAIR - BELOW))
-        pl.when(q == 3)(lambda: act(CHUNK - BELOW - 2 * BINS, 0, PAIR - ABOVE))
-        middle = jnp.logical_and(q > 0, q < 3)
-        pl.when(middle)(lambda: act(pl.multiple_of(2 * BINS * q - BELOW, 8), 0, PAIR))
+    def each_main(t, qs, act, local):
+        for q in qs:
+            if t < CHUNKS - 1:
+                act(main_copy(t, q))
+            else:
+                pl.when(q_me != q)(functools.partial(lambda q: act(main_copy(t, q)), q))
+                if local:
+                    pl.when(q_me == q)(functools.partial(lambda q: local(main_own(q)), q))
+
+    def on_window(act):
+        for q in range(4):
+            pl.when(q_me == q)(functools.partial(lambda q: act(*window(q)), q))
 
     def halo_targets(chunk):
         down_chip = lax.rem(4 * chunk + CHIPS - 1, CHIPS)
@@ -494,68 +516,62 @@
             t_ref.at[t, pl.ds(src, size)], g_ref.at[chip, pl.ds(dst, size)], h_recv.at[y]
         )
 
-    def each_halo(t, remote, local):
+    def each_halo(t, whichs, act, local):
         down_plane, down_chip, up_plane, up_chip = halo_targets(chunk_of(t))
         for which, plane, to in ((0, down_plane, down_chip), (1, up_plane, up_chip)):
+            if which not in whichs:
+                continue
             inside = jnp.logical_and(plane >= 0, plane < PLANES)
             me = jnp.logical_and(plane == z, to == chip)
             pl.when(jnp.logical_and(inside, jnp.logical_not(me)))(
-                functools.partial(remote, t, which, plane, to)
+                functools.partial(lambda *a: act(halo_copy(*a)), t, which, plane, to)
             )
-            pl.when(me)(functools.partial(local, t, which))
-
-    def each_main(t, act):
-        for off in range(4):
-            q = lax.rem(q_me + off, 4)
-            to_me = jnp.logical_and(t == CHUNKS - 1, off == 0)
-
-            def remote(q=q):
-                windows(q, functools.partial(act, t, q))
-
-            pl.when(jnp.logical_not(to_me))(remote)
-
-    def wait_block(block, _):
-        wait_for(z_ref.at[block], z_recv.at[block])
-        return 0
-
-    def sent_chunk(t, _):
-        each_main(t, lambda *a: main_copy(*a).wait_send())
-        each_halo(t, lambda *a: halo_copy(*a).wait_send(), lambda *a: None)
-        return 0
-
-    def plane_step(t, _):
-        @pl.when(t == 0)
-        def _():
-            lax.fori_loop(0, 3, wait_block, 0)
-
-        @pl.when(t == 2)
-        def _():
-            lax.fori_loop(0, 2, sent_chunk, 0)
-            wait_block(3, 0)
-
-        pair = lax.div(t, 2)
-        half = lax.rem(t, 2)
+            if local:
+                pl.when(me)(functools.partial(lambda *a: local(halo_mine(*a)), t, which))
+
+    def wait_block(block):
+        wait_for(zs[block], z_recv.at[block])
+
+    def start(copy):
+        copy.start()
+
+    def sent_chunk(t):
+        each_main(t, range(4), lambda copy: copy.wait_send(), None)
+        each_halo(t, (0, 1), lambda copy: copy.wait_send(), None)
+
+    def turn_chunk(t, rows):
         chunk = chunk_of(t)
-        for row in range(CHUNK_ROWS):
+        for row in rows:
             parts = []
             for c in range(2):
                 for r in range(2):
-                    start = size * chunk + CHUNK_ROWS * c + row
-                    parts.append(z_ref[r, pl.ds(start, PLANES, stride=PIECE), :])
-                for r in range(2):
-                    start = size * (2 * half + r) + CHUNK_ROWS * c + row
-                    parts.append(z_ref[2 + pair, pl.ds(start, PLANES, stride=PIECE), :])
+                    place = size * chunk + CHUNK_ROWS * c + row
+                    parts.append(zs[r][pl.ds(place, PLANES, stride=BLOCKS[r]), :])
+                for r in (2, 3):
+                    block, place = place_of(t, r, c, row)
+                    parts.append(zs[block][pl.ds(place, PLANES, stride=BLOCKS[block]), :])
             t_ref[t, LANES * row : LANES * (row + 1), :] = times_right(
                 jnp.concatenate(parts, axis=0).T, planes[...]
             )
-        each_main(t, lambda *a: main_copy(*a).start())
-
-        each_halo(t, lambda *a: halo_copy(*a).start(), lambda *a: halo_mine(*a).start())
-        return 0
-
-    lax.fori_loop(0, CHUNKS, plane_step, 0)
-
-    windows(q_me, lambda *a: main_own(*a).start())
+
+    for block in range(3):
+        wait_block(block)
+    for t in range(2):
+        turn_chunk(t, range(CHUNK_ROWS))
+        each_main(t, range(4), start, start)
+        each_halo(t, (0, 1), start, start)
+    turn_chunk(2, range(2))
+    each_main(2, (0, 1), start, start)
+    each_halo(2, (0,), start, start)
+    for t in range(2):
+        sent_chunk(t)
+    wait_block(3)
+    turn_chunk(2, (2,))
+    each_main(2, (2, 3), start, start)
+    each_halo(2, (1,), start, start)
+    turn_chunk(3, range(CHUNK_ROWS))
+    each_main(3, range(4), start, start)
+    each_halo(3, (0, 1), start, start)
 
     def core_copy(row):
         return pltpu.make_async_remote_copy(
@@ -570,19 +586,19 @@
     takes_up = jnp.logical_and(q_me == 0, jnp.logical_or(y > 0, has_below))
     takes_down = jnp.logical_and(q_me == 3, jnp.logical_or(y < 3, has_above))
 
-    def gather(t, _):
-        row = lax.rem(y + CHUNKS - chunk_of(t) + y, CHUNKS)
-
-        def rows_of(start, size):
-            return g_ref.at[pl.ds(4 * row, 4), pl.ds(start, size)]
-
-        windows(q_me, lambda src, dst, size: wait_for(rows_of(dst, size), p_recv.at[row]))
+    def gather(t):
+        row = lax.rem(2 * y + CHUNKS - chunk_of(t), CHUNKS)
+
+        def rows_of(first_row, count):
+            return g_ref.at[pl.ds(4 * row, 4), pl.ds(first_row, count)]
+
+        on_window(lambda src, dst, count: wait_for(rows_of(dst, count), p_recv.at[row]))
         pl.when(takes_up)(lambda: wait_for(rows_of(0, BELOW), h_recv.at[row]))
         pl.when(takes_down)(lambda: wait_for(rows_of(PAIR - ABOVE, ABOVE), h_recv.at[row]))
         core_copy(row).start()
-        return 0
-
-    lax.fori_loop(0, CHUNKS, gather, 0)
+
+    for t in range(CHUNKS):
+        gather(t)
 
     part = WINDOW // 2
 
@@ -621,9 +637,9 @@
         core_copy(row).wait_recv()
         return 0
 
-    lax.fori_loop(2, 4, sent_chunk, 0)
-    for block in (2, 3):
-        sent_block(block)
+    for t in (2, 3):
+        sent_chunk(t)
+    sent_block(3)
     lax.fori_loop(0, 4, wait_core, 0)
     turn_rows(lambda k, start: o_ref[k, pl.ds(pl.multiple_of(start, 8), part), :])
     transform(1 - core, True)
@@ -673,19 +689,30 @@
         result_copy(step).wait()
 
 
-FINISH_ROWS = 16
-
-
-def finish_kernel(f_ref, out_ref):
-    for half in range(FINISH_ROWS // 8):
-        rows = slice(8 * half, 8 * (half + 1))
+def finish_kernel(f_hbm, out_hbm, f_ref, out_ref, in_sem, out_sem):
+    def fetch(step):
+        rows = slice(8 * step, 8 * (step + 1))
+        return pltpu.make_async_copy(f_hbm.at[:, :, rows], f_ref.at[:, :, rows], in_sem.at[step])
+
+    def store(step):
+        rows = slice(8 * step, 8 * (step + 1))
+        return pltpu.make_async_copy(out_ref.at[:, rows], out_hbm.at[:, rows], out_sem.at[step])
+
+    for step in range(BINS // 8):
+        fetch(step).start()
+    for step in range(BINS // 8):
+        rows = slice(8 * step, 8 * (step + 1))
+        fetch(step).wait()
         got = fft_list([(f_ref[0, k1, rows, :], f_ref[1, k1, rows, :]) for k1 in range(16)], 1)
         for tile in range(16):
             for c in range(2):
                 out_ref[c, rows, LANES * tile : LANES * (tile + 1)] = got[tile][c]
-
-
-ANY = pl.BlockSpec(memory_space=pl.ANY)
+        store(step).start()
+    for step in range(BINS // 8):
+        store(step).wait()
+
+
+IN_HBM = pl.BlockSpec(memory_space=pltpu.HBM)
 DMA = pltpu.SemaphoreType.DMA
 
 
@@ -722,12 +749,11 @@
         pltpu.VMEM((LANE_PULSES, 2, 48, LANES), F32),
         pltpu.VMEM((LANE_PULSES, 2, 48, LANES), F32),
         pltpu.VMEM((LANE_PULSES, 2, 48, LANES), F32),
-        pltpu.VMEM((LANE_PULSES, 2, 48, LANES), F32),
         pltpu.VMEM((LANE_PULSES, 2, ROWS, LANES), F32),
         pltpu.VMEM((2, ROWS, LANES), F32),
         pltpu.VMEM((LANE_PULSES, 6 * ROWS, LANES), BF16),
-        pltpu.VMEM((CHUNKS, PLANES, PIECE, LANES), F32),
-        pltpu.VMEM((CHUNKS, PLANES * PIECE, LANES), F32),
+        *[pltpu.VMEM((PLANES, rows, LANES), F32) for rows in BLOCKS],
+        *[pltpu.VMEM((PLANES * rows, LANES), F32) for rows in BLOCKS],
         pltpu.VMEM((CHUNKS, CHUNK, LANES), F32),
         pltpu.VMEM((CHIPS, PAIR, LANES), F32),
         pltpu.VMEM((CHIPS, WINDOW, LANES), F32),
@@ -739,15 +765,15 @@
         pltpu.VMEM((4, 2, WINDOW, LANES), F32),
         pltpu.VMEM((4, 2, WINDOW, LANES), F32),
         pltpu.VMEM((2, 16, BINS, LANES), F32),
-        DMA((2,)), DMA((4, 2)), DMA((4, 2)), DMA((4, 2)), DMA((4, 2)),
+        DMA((2,)), DMA((4, 3)), DMA((4, 3)),
         DMA((4,)), DMA((4,)),
         DMA((CHUNKS, 4)), DMA((4,)), DMA((CHUNKS, 2)), DMA((4,)), DMA((4,)), DMA((4,)), DMA((4,)),
     ]
     turned = pl.pallas_call(
         kernel,
         out_shape=jax.ShapeDtypeStruct((2, 16, BINS, LANES), F32),
-        in_specs=[ANY] * (len(operands) + len(tables)),
-        out_specs=ANY,
+        in_specs=[IN_HBM] * (len(operands) + len(tables)),
+        out_specs=IN_HBM,
         scratch_shapes=loads + [DMA((len(loads),))] + scratch,
         compiler_params=pltpu.CompilerParams(
             vmem_limit_bytes=60 * 2**20, collective_id=0, has_side_effects=True
@@ -756,9 +782,15 @@
     return pl.pallas_call(
         finish_kernel,
         out_shape=jax.ShapeDtypeStruct((2, BINS, PULSES), F32),
-        grid=(BINS // FINISH_ROWS,),
-        in_specs=[pl.BlockSpec((2, 16, FINISH_ROWS, LANES), lambda i: (0, 0, i, 0))],
-        out_specs=pl.BlockSpec((2, FINISH_ROWS, PULSES), lambda i: (0, i, 0)),
+        in_specs=[IN_HBM],
+        out_specs=IN_HBM,
+        scratch_shapes=[
+            pltpu.VMEM((2, 16, BINS, LANES), F32),
+            pltpu.VMEM((2, BINS, PULSES), F32),
+            DMA((BINS // 8,)),
+            DMA((BINS // 8,)),
+        ],
+        compiler_params=pltpu.CompilerParams(vmem_limit_bytes=60 * 2**20),
     )(turned)
 
 

time: 78.9 us -> 80.1 us (1.015)
  Pallas kernels: 77.6 us -> 78.6 us
    pallas_call x1, Pallas kernels: 74.6 us -> 76.6 us  [shards(): pl.pallas_call(kernel, out_shape=jax.ShapeDtypeStruct((2, 16, BINS, LANES...]
    pallas_call x1, Pallas kernels: 2.95 us -> 2 us  [shards(): pl.pallas_call(finish_kernel, out_shape=jax.ShapeDtypeStruct((2, BINS, PU...]
where the time goes in v5:
time: 80.1 us; the launch traced here: 78.6 us
  Pallas kernels  78.6 us (98%)
    pallas_call x1, Pallas kernels, shards(): pl.pallas_call(kernel, out_shape=jax.ShapeDtypeStruct((2, 16, BINS, LANES...  76.6 us
    pallas_call x1, Pallas kernels, shards(): pl.pallas_call(finish_kernel, out_shape=jax.ShapeDtypeStruct((2, BINS, PU...  2 us

profile of v5, /device:TPU:1, one launch (start us, length us, event | category | flops | bytes accessed | tf_op | source)
XLA Modules:
  0.0 78.6 jit_solution(11474445727101059321)
XLA Ops:
  0.0 76.6 %shard_map.145.f_hbm = f32[2,16,48,128]{3,2,1,0:T(8,128)} custom-call(f32[2,2,384,128]{3,2,1,0:T(8,128)} %bitcast.13, f32[384,128]{1,0:T(8,128)} %bitcast.14, f32[2,48,2048]{2,1,0:T(8,128)} %azf_hbm.1, s32[16,128]{1,0:T(8,128)} %bitcast.15, s32[16,128]{1,0:T(8,128)} %bitcast.16, f32[8,16]{1,0:T(8,128)} %bitcast.17, ...), custom_call_target="tpu_custom_call" | custom-call | tf_op jit(solution)/shard_map/pallas_call | solution.py:772
  76.6 2.0 %shard_map.146 = f32[2,48,2048]{2,1,0:T(8,128)} custom-call(f32[2,16,48,128]{3,2,1,0:T(8,128)} %shard_map.145.f_hbm), custom_call_target="tpu_custom_call" | custom-call | tf_op jit(solution)/shard_map/pallas_call | solution.py:782

commit v6 on v4

--- a/solution.py
+++ b/solution.py
@@ -32,6 +32,7 @@
 WINDOW = BELOW + BINS + ABOVE
 PAIR = BELOW + 2 * BINS + ABOVE
 TAPS = 8
+NEAR = 4
 ORDER = ((2, 1, 3, 0), (2, 3, 1, 0))
 
 
@@ -187,9 +188,9 @@
     out_hbm,
     filt_in, azf_in, shift_in, frac_in, ktab, first, last, twist, fwd, back, planes, az_fwd, az_back, az_twist,
     load_sem,
-    tiles, to_like, to_relay, relay, to_core, x_ref, filt, v_ref, y_ref, z_ref, t_ref, g_ref, o_ref,
+    tiles, to_like, to_cross, to_core, x_ref, filt, v_ref, y_ref, z_ref, t_ref, g_ref, o_ref,
     shift_ref, w_ref, a_ref, h_ref, d_ref, m_ref, e_ref, f_ref,
-    tile_sem, x_send, x_recv, core_send, core_recv, z_send, z_recv,
+    tile_sem, x_send, x_recv, z_send, z_recv,
     p_send, p_recv, h_send, h_recv, fwd_send, fwd_recv, out_sem,
 ):
     pulse = lax.axis_index("pulse")
@@ -207,6 +208,7 @@
         return (8 * plane + lax.div(other_chip, 2), 2 * lax.rem(other_chip, 2) + other_core)
 
     x_partner = (pulse, 2 * (1 - xh) + core)
+    x_cross = (pulse, 2 * (1 - xh) + 1 - core)
     core_partner = (pulse, 2 * xh + 1 - core)
 
     place = 2 * chip + core
@@ -230,6 +232,7 @@
         pl.semaphore_signal(barrier, inc=1, device_id=to, device_id_type=MESH)
 
     greet(x_partner)
+    greet(x_cross)
     greet(core_partner)
 
     def greet_z(off, _):
@@ -266,7 +269,6 @@
     pl.when(jnp.logical_and(chip == CHIPS - 1, z == PLANES - 1))(lambda: blank(PAIR - ABOVE, ABOVE))
 
     my_quarter = 2 * xh + core
-    x_quarter = 2 * (1 - xh) + core
 
     def quarter_rows(quarter):
         return pl.ds(pl.multiple_of(48 * quarter, 8), 48)
@@ -278,40 +280,29 @@
         other = pl.ds(4 * (1 - core) + r, 48, stride=8)
         for c in range(2):
             to_like[r, c] = tiles[1, c, like, :]
-            to_relay[r, c] = tiles[1, c, other, :]
+            to_cross[r, c] = tiles[1, c, other, :]
             to_core[r, c] = tiles[0, c, other, :]
             x_ref[r, c, quarter_rows(my_quarter), :] = tiles[0, c, like, :]
 
     sort_pulse(0)
     pl.semaphore_wait(
         barrier,
-        2 + PLANES - 1 + CHIPS - 1 + jnp.where(has_below, 1, 0) + jnp.where(has_above, 1, 0),
+        3 + PLANES - 1 + CHIPS - 1 + jnp.where(has_below, 1, 0) + jnp.where(has_above, 1, 0),
     )
 
-    def x_copy(r, which):
+    def pulse_copy(r, which):
         return pltpu.make_async_remote_copy(
-            src_ref=(to_like, to_relay)[which].at[r],
-            dst_ref=x_ref.at[r, :, quarter_rows(my_quarter)] if which == 0 else relay.at[r],
+            src_ref=(to_like, to_cross, to_core)[which].at[r],
+            dst_ref=x_ref.at[r, :, quarter_rows(my_quarter)],
             send_sem=x_send.at[r, which],
             recv_sem=x_recv.at[r, which],
-            device_id=x_partner,
+            device_id=(x_partner, x_cross, core_partner)[which],
             device_id_type=MESH,
         )
 
-    def core_swap(r, which):
-        return pltpu.make_async_remote_copy(
-            src_ref=(to_core, relay)[which].at[r],
-            dst_ref=x_ref.at[r, :, quarter_rows((my_quarter, x_quarter)[which])],
-            send_sem=core_send.at[r, which],
-            recv_sem=core_recv.at[r, which],
-            device_id=core_partner,
-            device_id_type=MESH,
-        )
-
     def send_pulse(r):
-        x_copy(r, 1).start()
-        x_copy(r, 0).start()
-        core_swap(r, 0).start()
+        for which in range(3):
+            pulse_copy(r, which).start()
 
     send_pulse(0)
     for r in range(1, LANE_PULSES):
@@ -325,12 +316,9 @@
         filt[c] = jnp.concatenate([tall[:ROWS], tall[ROWS:]], axis=1)
 
     def compress(r):
-        x_copy(r, 1).wait_recv()
-        core_swap(r, 1).start()
-        x_copy(r, 0).wait_recv()
+        for which in range(3):
+            pulse_copy(r, which).wait_recv()
         pl.when(r < LANE_PULSES - 1)(lambda: send_pulse(r + 1))
-        core_swap(r, 0).wait_recv()
-        core_swap(r, 1).wait_recv()
         twist_re, twist_im = twist[0], twist[1]
         v = times_left(first[...], jnp.concatenate([x_ref[r, 0], x_ref[r, 1]], axis=0))
         re, im = cmul(v[:ROWS], v[ROWS:], twist_re, twist_im)
@@ -364,16 +352,26 @@
             y_ref.at[block, z], z_ref.at[block, pl.ds(pl.multiple_of(PIECE * z, 8), PIECE)], z_recv.at[block]
         )
 
-    def send_block(block):
+    def send_to(block, first, last):
         def start(step, _):
-            near = PLANES // 2 - step
+            near = last - step
             z_copy(block, near).start()
             z_copy(block, PLANES - near).start()
             return 0
 
+        lax.fori_loop(0, last - first + 1, start, 0)
+
+    def send_far(block):
         z_copy(block, PLANES // 2).start()
-        lax.fori_loop(1, PLANES // 2, start, 0)
+        send_to(block, NEAR + 1, PLANES // 2 - 1)
         z_mine(block).start()
+
+    def send_near(block):
+        send_to(block, 1, NEAR)
+
+    def send_block(block):
+        send_far(block)
+        send_near(block)
 
     def wait_for(ref, sem):
         pltpu.make_async_copy(ref, ref, sem).wait()
@@ -435,16 +433,15 @@
         w_ref[tap] = weight
 
     for r in range(LANE_PULSES):
-        for which in range(2):
-            x_copy(r, which).wait_send()
-            core_swap(r, which).wait_send()
-
-    def next_block(block, _):
-        sent_block(block)
-        send_block(block + 2)
-        return 0
-
-    lax.fori_loop(0, 2, next_block, 0)
+        for which in range(3):
+            pulse_copy(r, which).wait_send()
+
+    sent_block(0)
+    send_block(2)
+    sent_block(1)
+    send_far(3)
+    sent_block(2)
+    send_near(3)
 
     def main_copy(t, q, src, dst, size):
         return pltpu.make_async_remote_copy(
@@ -622,8 +619,7 @@
         return 0
 
     lax.fori_loop(2, 4, sent_chunk, 0)
-    for block in (2, 3):
-        sent_block(block)
+    sent_block(3)
     lax.fori_loop(0, 4, wait_core, 0)
     turn_rows(lambda k, start: o_ref[k, pl.ds(pl.multiple_of(start, 8), part), :])
     transform(1 - core, True)
@@ -673,19 +669,30 @@
         result_copy(step).wait()
 
 
-FINISH_ROWS = 16
-
-
-def finish_kernel(f_ref, out_ref):
-    for half in range(FINISH_ROWS // 8):
-        rows = slice(8 * half, 8 * (half + 1))
+def finish_kernel(f_hbm, out_hbm, f_ref, out_ref, in_sem, out_sem):
+    def fetch(step):
+        rows = slice(8 * step, 8 * (step + 1))
+        return pltpu.make_async_copy(f_hbm.at[:, :, rows], f_ref.at[:, :, rows], in_sem.at[step])
+
+    def store(step):
+        rows = slice(8 * step, 8 * (step + 1))
+        return pltpu.make_async_copy(out_ref.at[:, rows], out_hbm.at[:, rows], out_sem.at[step])
+
+    for step in range(BINS // 8):
+        fetch(step).start()
+    for step in range(BINS // 8):
+        rows = slice(8 * step, 8 * (step + 1))
+        fetch(step).wait()
         got = fft_list([(f_ref[0, k1, rows, :], f_ref[1, k1, rows, :]) for k1 in range(16)], 1)
         for tile in range(16):
             for c in range(2):
                 out_ref[c, rows, LANES * tile : LANES * (tile + 1)] = got[tile][c]
-
-
-ANY = pl.BlockSpec(memory_space=pl.ANY)
+        store(step).start()
+    for step in range(BINS // 8):
+        store(step).wait()
+
+
+IN_HBM = pl.BlockSpec(memory_space=pltpu.HBM)
 DMA = pltpu.SemaphoreType.DMA
 
 
@@ -722,7 +729,6 @@
         pltpu.VMEM((LANE_PULSES, 2, 48, LANES), F32),
         pltpu.VMEM((LANE_PULSES, 2, 48, LANES), F32),
         pltpu.VMEM((LANE_PULSES, 2, 48, LANES), F32),
-        pltpu.VMEM((LANE_PULSES, 2, 48, LANES), F32),
         pltpu.VMEM((LANE_PULSES, 2, ROWS, LANES), F32),
         pltpu.VMEM((2, ROWS, LANES), F32),
         pltpu.VMEM((LANE_PULSES, 6 * ROWS, LANES), BF16),
@@ -739,15 +745,15 @@
         pltpu.VMEM((4, 2, WINDOW, LANES), F32),
         pltpu.VMEM((4, 2, WINDOW, LANES), F32),
         pltpu.VMEM((2, 16, BINS, LANES), F32),
-        DMA((2,)), DMA((4, 2)), DMA((4, 2)), DMA((4, 2)), DMA((4, 2)),
+        DMA((2,)), DMA((4, 3)), DMA((4, 3)),
         DMA((4,)), DMA((4,)),
         DMA((CHUNKS, 4)), DMA((4,)), DMA((CHUNKS, 2)), DMA((4,)), DMA((4,)), DMA((4,)), DMA((4,)),
     ]
     turned = pl.pallas_call(
         kernel,
         out_shape=jax.ShapeDtypeStruct((2, 16, BINS, LANES), F32),
-        in_specs=[ANY] * (len(operands) + len(tables)),
-        out_specs=ANY,
+        in_specs=[IN_HBM] * (len(operands) + len(tables)),
+        out_specs=IN_HBM,
         scratch_shapes=loads + [DMA((len(loads),))] + scratch,
         compiler_params=pltpu.CompilerParams(
             vmem_limit_bytes=60 * 2**20, collective_id=0, has_side_effects=True
@@ -756,9 +762,15 @@
     return pl.pallas_call(
         finish_kernel,
         out_shape=jax.ShapeDtypeStruct((2, BINS, PULSES), F32),
-        grid=(BINS // FINISH_ROWS,),
-        in_specs=[pl.BlockSpec((2, 16, FINISH_ROWS, LANES), lambda i: (0, 0, i, 0))],
-        out_specs=pl.BlockSpec((2, FINISH_ROWS, PULSES), lambda i: (0, i, 0)),
+        in_specs=[IN_HBM],
+        out_specs=IN_HBM,
+        scratch_shapes=[
+            pltpu.VMEM((2, 16, BINS, LANES), F32),
+            pltpu.VMEM((2, BINS, PULSES), F32),
+            DMA((BINS // 8,)),
+            DMA((BINS // 8,)),
+        ],
+        compiler_params=pltpu.CompilerParams(vmem_limit_bytes=60 * 2**20),
     )(turned)
 
 

time: 78.9 us -> 76.5 us (0.970)
  Pallas kernels: 77.6 us -> 75.9 us
    pallas_call x1, Pallas kernels: 2.95 us -> 2 us  [shards(): pl.pallas_call(finish_kernel, out_shape=jax.ShapeDtypeStruct((2, BINS, PU...]
where the time goes in v6:
time: 76.5 us; the launch traced here: 75.9 us
  Pallas kernels  75.9 us (99%)
    pallas_call x1, Pallas kernels, shards(): pl.pallas_call(kernel, out_shape=jax.ShapeDtypeStruct((2, 16, BINS, LANES...  73.9 us
    pallas_call x1, Pallas kernels, shards(): pl.pallas_call(finish_kernel, out_shape=jax.ShapeDtypeStruct((2, BINS, PU...  2 us

profile of v6, /device:TPU:1, one launch (start us, length us, event | category | flops | bytes accessed | tf_op | source)
XLA Modules:
  0.0 75.9 jit_solution(16541806200295794978)
XLA Ops:
  0.0 73.9 %shard_map.145.f_hbm = f32[2,16,48,128]{3,2,1,0:T(8,128)} custom-call(f32[2,2,384,128]{3,2,1,0:T(8,128)} %bitcast.13, f32[384,128]{1,0:T(8,128)} %bitcast.14, f32[2,48,2048]{2,1,0:T(8,128)} %azf_hbm.1, s32[16,128]{1,0:T(8,128)} %bitcast.15, s32[16,128]{1,0:T(8,128)} %bitcast.16, f32[8,16]{1,0:T(8,128)} %bitcast.17, ...), custom_call_target="tpu_custom_call" | custom-call | tf_op jit(solution)/shard_map/pallas_call | solution.py:752
  73.9 2.0 %shard_map.146 = f32[2,48,2048]{2,1,0:T(8,128)} custom-call(f32[2,16,48,128]{3,2,1,0:T(8,128)} %shard_map.145.f_hbm), custom_call_target="tpu_custom_call" | custom-call | tf_op jit(solution)/shard_map/pallas_call | solution.py:762

commit v7 on v5

--- a/solution.py
+++ b/solution.py
@@ -26,13 +26,12 @@
 CHUNKS = 4
 CHUNK_ROWS = 3
 CHUNK = CHUNK_ROWS * LANES
-BLOCKS = (24, 24, 32, 16)
+BLOCKS = (24, 24, 16, 16, 16)
 BELOW = 8
 ABOVE = 24
 WINDOW = BELOW + BINS + ABOVE
 PAIR = BELOW + 2 * BINS + ABOVE
 TAPS = 8
-NEAR = 4
 ORDER = ((2, 1, 3, 0), (2, 3, 1, 0))
 
 
@@ -188,7 +187,7 @@
     out_hbm,
     filt_in, azf_in, shift_in, frac_in, ktab, first, last, twist, fwd, back, planes, az_fwd, az_back, az_twist,
     load_sem,
-    tiles, to_like, to_cross, to_core, x_ref, filt, v_ref, y0, y1, y2, y3, z0, z1, z2, z3, t_ref, g_ref, o_ref,
+    tiles, to_like, to_cross, to_core, x_ref, filt, v_ref, y0, y1, y2, y3, y4, z0, z1, z2, z3, z4, t_ref, g_ref, o_ref,
     shift_ref, w_ref, a_ref, h_ref, d_ref, m_ref, e_ref, f_ref,
     tile_sem, x_send, x_recv, z_send, z_recv,
     p_send, p_recv, h_send, h_recv, fwd_send, fwd_recv, out_sem,
@@ -315,10 +314,11 @@
         tall = jnp.concatenate(cols, axis=0)
         filt[c] = jnp.concatenate([tall[:ROWS], tall[ROWS:]], axis=1)
 
-    def compress(r):
+    def wait_pulse(r):
         for which in range(3):
             pulse_copy(r, which).wait_recv()
-        pl.when(r < LANE_PULSES - 1)(lambda: send_pulse(r + 1))
+
+    def compress(r):
         twist_re, twist_im = twist[0], twist[1]
         v = times_left(first[...], jnp.concatenate([x_ref[r, 0], x_ref[r, 1]], axis=0))
         re, im = cmul(v[:ROWS], v[ROWS:], twist_re, twist_im)
@@ -331,7 +331,7 @@
         v_ref[r, 2 * ROWS : 4 * ROWS] = low
         v_ref[r, 4 * ROWS : 6 * ROWS] = high
 
-    ys, zs = (y0, y1, y2, y3), (z0, z1, z2, z3)
+    ys, zs = (y0, y1, y2, y3, y4), (z0, z1, z2, z3, z4)
 
     def chunk_of(t):
         if t in (0, 3):
@@ -355,26 +355,16 @@
     def z_mine(block):
         return pltpu.make_async_copy(ys[block].at[z], zs[block].at[z_mine_rows(block)], z_recv.at[block])
 
-    def send_to(block, first, last):
+    def send_block(block):
         def start(step, _):
-            near = last - step
+            near = PLANES // 2 - step
             z_copy(block, near).start()
             z_copy(block, PLANES - near).start()
             return 0
 
-        lax.fori_loop(0, last - first + 1, start, 0)
-
-    def send_far(block):
         z_copy(block, PLANES // 2).start()
-        send_to(block, NEAR + 1, PLANES // 2 - 1)
+        lax.fori_loop(1, PLANES // 2, start, 0)
         z_mine(block).start()
-
-    def send_near(block):
-        send_to(block, 1, NEAR)
-
-    def send_block(block):
-        send_far(block)
-        send_near(block)
 
     def wait_for(ref, sem):
         pltpu.make_async_copy(ref, ref, sem).wait()
@@ -385,15 +375,15 @@
     size = 2 * CHUNK_ROWS
 
     def place_of(t, r, c, row):
-        if t == 3:
-            return 3, 6 * (r - 2) + 3 * c + row
-        if t < 2:
-            return 2, 12 * t + 6 * (r - 2) + 3 * c + row
-        if row < 2:
-            return 2, 24 + 4 * (r - 2) + 2 * c + row
-        return 3, 12 + 2 * (r - 2) + c
+        rows = {0: (0, 1, 2), 1: (0,) if row == 0 else (1, 2), 2: (0, 1) if row < 2 else (2,), 3: (0, 1, 2)}[t]
+        block, start = {(0, 0): (2, 0), (1, 0): (2, 12), (1, 1): (3, 0), (2, 0): (3, 8), (2, 2): (4, 0), (3, 0): (4, 4)}[
+            t, rows[0]
+        ]
+        return block, start + len(rows) * (2 * (r - 2) + c) + row - rows[0]
 
     for r in range(2):
+        wait_pulse(r)
+        send_pulse(r + 1)
         compress(r)
         for chunk in range(CHUNKS):
             out = jnp.dot(last[chunk], v_ref[r], preferred_element_type=F32)
@@ -402,22 +392,32 @@
         send_block(r)
 
     def later_pulse(r, _):
+        wait_pulse(r)
+        pl.when(r < LANE_PULSES - 1)(lambda: send_pulse(r + 1))
         compress(r)
         return 0
 
     lax.fori_loop(2, 4, later_pulse, 0)
     both = jnp.concatenate([v_ref[2], v_ref[3]], axis=1)
-    for t in range(CHUNKS):
+
+    def make_chunk(t):
         out = jnp.dot(last[chunk_of(t)], both, preferred_element_type=F32)
         for r in (2, 3):
             lanes = slice(LANES * (r - 2), LANES * (r - 1))
-            pieces = [(0, 6)] if t != 2 else [(0, 2), (2, 3), (3, 5), (5, 6)]
+            pieces = {1: [(0, 1), (1, 3), (3, 4), (4, 6)], 2: [(0, 2), (2, 3), (3, 5), (5, 6)]}.get(t, [(0, 6)])
             for first_row, end in pieces:
                 block, place = place_of(t, r, first_row // 3, first_row % 3)
                 for to in range(PLANES):
                     ys[block][to, place : place + end - first_row, :] = out[
                         size * to + first_row : size * to + end, lanes
                     ]
+
+    for t in range(2):
+        make_chunk(t)
+    sent_block(0)
+    send_block(2)
+    for t in (2, 3):
+        make_chunk(t)
 
     def turn_filter(step, _):
         rows = pl.ds(pl.multiple_of(8 * step, 8), 8)
@@ -445,12 +445,10 @@
         for which in range(3):
             pulse_copy(r, which).wait_send()
 
-    sent_block(0)
-    send_block(2)
     sent_block(1)
-    send_far(3)
+    send_block(3)
     sent_block(2)
-    send_near(3)
+    send_block(4)
 
     def window(q):
         if q == 0:
@@ -556,16 +554,18 @@
 
     for block in range(3):
         wait_block(block)
-    for t in range(2):
-        turn_chunk(t, range(CHUNK_ROWS))
-        each_main(t, range(4), start, start)
-        each_halo(t, (0, 1), start, start)
+    turn_chunk(0, range(CHUNK_ROWS))
+    each_main(0, range(4), start, start)
+    each_halo(0, (0, 1), start, start)
+    wait_block(3)
+    turn_chunk(1, range(CHUNK_ROWS))
+    each_main(1, range(4), start, start)
+    each_halo(1, (0, 1), start, start)
     turn_chunk(2, range(2))
     each_main(2, (0, 1), start, start)
     each_halo(2, (0,), start, start)
-    for t in range(2):
-        sent_chunk(t)
-    wait_block(3)
+    sent_chunk(0)
+    wait_block(4)
     turn_chunk(2, (2,))
     each_main(2, (2, 3), start, start)
     each_halo(2, (1,), start, start)
@@ -637,9 +637,10 @@
         core_copy(row).wait_recv()
         return 0
 
-    for t in (2, 3):
+    for t in (1, 2, 3):
         sent_chunk(t)
     sent_block(3)
+    sent_block(4)
     lax.fori_loop(0, 4, wait_core, 0)
     turn_rows(lambda k, start: o_ref[k, pl.ds(pl.multiple_of(start, 8), part), :])
     transform(1 - core, True)
@@ -766,7 +767,7 @@
         pltpu.VMEM((4, 2, WINDOW, LANES), F32),
         pltpu.VMEM((2, 16, BINS, LANES), F32),
         DMA((2,)), DMA((4, 3)), DMA((4, 3)),
-        DMA((4,)), DMA((4,)),
+        DMA((len(BLOCKS),)), DMA((len(BLOCKS),)),
         DMA((CHUNKS, 4)), DMA((4,)), DMA((CHUNKS, 2)), DMA((4,)), DMA((4,)), DMA((4,)), DMA((4,)),
     ]
     turned = pl.pallas_call(

time: 80.1 us -> 74 us (0.924); the launches traced: 78.6 us -> 73.5 us
  Pallas kernels: 78.6 us -> 73.5 us
    pallas_call x1, Pallas kernels: 76.6 us -> 71.5 us  [shards(): pl.pallas_call(kernel, out_shape=jax.ShapeDtypeStruct((2, 16, BINS, LANES...]
where the time goes in v7:
time: 74 us; the launch traced here: 73.5 us
  Pallas kernels  73.5 us (99%)
    pallas_call x1, Pallas kernels, shards(): pl.pallas_call(kernel, out_shape=jax.ShapeDtypeStruct((2, 16, BINS, LANES...  71.5 us
    pallas_call x1, Pallas kernels, shards(): pl.pallas_call(finish_kernel, out_shape=jax.ShapeDtypeStruct((2, BINS, PU...  2 us

profile of v7, /device:TPU:1, one launch (start us, length us, event | category | flops | bytes accessed | tf_op | source)
XLA Modules:
  0.0 73.5 jit_solution(10356124434956262285)
XLA Ops:
  0.0 71.5 %shard_map.145.f_hbm = f32[2,16,48,128]{3,2,1,0:T(8,128)} custom-call(f32[2,2,384,128]{3,2,1,0:T(8,128)} %bitcast.13, f32[384,128]{1,0:T(8,128)} %bitcast.14, f32[2,48,2048]{2,1,0:T(8,128)} %azf_hbm.1, s32[16,128]{1,0:T(8,128)} %bitcast.15, s32[16,128]{1,0:T(8,128)} %bitcast.16, f32[8,16]{1,0:T(8,128)} %bitcast.17, ...), custom_call_target="tpu_custom_call" | custom-call | tf_op jit(solution)/shard_map/pallas_call | solution.py:773
  71.5 2.0 %shard_map.146 = f32[2,48,2048]{2,1,0:T(8,128)} custom-call(f32[2,16,48,128]{3,2,1,0:T(8,128)} %shard_map.145.f_hbm), custom_call_target="tpu_custom_call" | custom-call | tf_op jit(solution)/shard_map/pallas_call | solution.py:783

commit v8 on v7

--- a/solution.py
+++ b/solution.py
@@ -26,7 +26,7 @@
 CHUNKS = 4
 CHUNK_ROWS = 3
 CHUNK = CHUNK_ROWS * LANES
-BLOCKS = (24, 24, 16, 16, 16)
+BLOCKS = (24, 24, 16, 16, 8, 8)
 BELOW = 8
 ABOVE = 24
 WINDOW = BELOW + BINS + ABOVE
@@ -187,7 +187,7 @@
     out_hbm,
     filt_in, azf_in, shift_in, frac_in, ktab, first, last, twist, fwd, back, planes, az_fwd, az_back, az_twist,
     load_sem,
-    tiles, to_like, to_cross, to_core, x_ref, filt, v_ref, y0, y1, y2, y3, y4, z0, z1, z2, z3, z4, t_ref, g_ref, o_ref,
+    tiles, to_like, to_cross, to_core, x_ref, filt, v_ref, y0, y1, y2, y3, y4, y5, z0, z1, z2, z3, z4, z5, t_ref, g_ref, o_ref,
     shift_ref, w_ref, a_ref, h_ref, d_ref, m_ref, e_ref, f_ref,
     tile_sem, x_send, x_recv, z_send, z_recv,
     p_send, p_recv, h_send, h_recv, fwd_send, fwd_recv, out_sem,
@@ -331,7 +331,7 @@
         v_ref[r, 2 * ROWS : 4 * ROWS] = low
         v_ref[r, 4 * ROWS : 6 * ROWS] = high
 
-    ys, zs = (y0, y1, y2, y3, y4), (z0, z1, z2, z3, z4)
+    ys, zs = (y0, y1, y2, y3, y4, y5), (z0, z1, z2, z3, z4, z5)
 
     def chunk_of(t):
         if t in (0, 3):
@@ -375,8 +375,10 @@
     size = 2 * CHUNK_ROWS
 
     def place_of(t, r, c, row):
-        rows = {0: (0, 1, 2), 1: (0,) if row == 0 else (1, 2), 2: (0, 1) if row < 2 else (2,), 3: (0, 1, 2)}[t]
-        block, start = {(0, 0): (2, 0), (1, 0): (2, 12), (1, 1): (3, 0), (2, 0): (3, 8), (2, 2): (4, 0), (3, 0): (4, 4)}[
+        rows = {0: (0, 1, 2), 1: (0,) if row == 0 else (1, 2), 2: (0, 1) if row < 2 else (2,)}
+        rows[3] = rows[1]
+        rows = rows[t]
+        block, start = {(0, 0): (2, 0), (1, 0): (2, 12), (1, 1): (3, 0), (2, 0): (3, 8), (2, 2): (4, 0), (3, 0): (4, 4), (3, 1): (5, 0)}[
             t, rows[0]
         ]
         return block, start + len(rows) * (2 * (r - 2) + c) + row - rows[0]
@@ -404,7 +406,9 @@
         out = jnp.dot(last[chunk_of(t)], both, preferred_element_type=F32)
         for r in (2, 3):
             lanes = slice(LANES * (r - 2), LANES * (r - 1))
-            pieces = {1: [(0, 1), (1, 3), (3, 4), (4, 6)], 2: [(0, 2), (2, 3), (3, 5), (5, 6)]}.get(t, [(0, 6)])
+            pieces = [(0, 6)] if t == 0 else [(0, 2), (2, 3), (3, 5), (5, 6)]
+            if t in (1, 3):
+                pieces = [(0, 1), (1, 3), (3, 4), (4, 6)]
             for first_row, end in pieces:
                 block, place = place_of(t, r, first_row // 3, first_row % 3)
                 for to in range(PLANES):
@@ -558,6 +562,8 @@
     each_main(0, range(4), start, start)
     each_halo(0, (0, 1), start, start)
     wait_block(3)
+    sent_block(3)
+    send_block(5)
     turn_chunk(1, range(CHUNK_ROWS))
     each_main(1, range(4), start, start)
     each_halo(1, (0, 1), start, start)
@@ -569,9 +575,13 @@
     turn_chunk(2, (2,))
     each_main(2, (2, 3), start, start)
     each_halo(2, (1,), start, start)
-    turn_chunk(3, range(CHUNK_ROWS))
-    each_main(3, range(4), start, start)
-    each_halo(3, (0, 1), start, start)
+    turn_chunk(3, (0,))
+    each_main(3, (0,), start, start)
+    each_halo(3, (0,), start, start)
+    wait_block(5)
+    turn_chunk(3, (1, 2))
+    each_main(3, (1, 2, 3), start, start)
+    each_halo(3, (1,), start, start)
 
     def core_copy(row):
         return pltpu.make_async_remote_copy(
@@ -639,8 +649,8 @@
 
     for t in (1, 2, 3):
         sent_chunk(t)
-    sent_block(3)
     sent_block(4)
+    sent_block(5)
     lax.fori_loop(0, 4, wait_core, 0)
     turn_rows(lambda k, start: o_ref[k, pl.ds(pl.multiple_of(start, 8), part), :])
     transform(1 - core, True)

time: 74 us -> 74.8 us (1.011)
  the two profiles are of different devices: /device:TPU:1 before, /device:TPU:33 now
where the time goes in v8:
time: 74.8 us; the launch traced here: 74.7 us
  Pallas kernels  74.7 us (100%)
    pallas_call x1, Pallas kernels, shards(): pl.pallas_call(kernel, out_shape=jax.ShapeDtypeStruct((2, 16, BINS, LANES...  72.7 us
    pallas_call x1, Pallas kernels, shards(): pl.pallas_call(finish_kernel, out_shape=jax.ShapeDtypeStruct((2, BINS, PU...  2 us

profile of v8, /device:TPU:33, one launch (start us, length us, event | category | flops | bytes accessed | tf_op | source)
XLA Modules:
  0.0 74.7 jit_solution(11609657385707492241)
XLA Ops:
  0.0 72.7 %shard_map.145.f_hbm = f32[2,16,48,128]{3,2,1,0:T(8,128)} custom-call(f32[2,2,384,128]{3,2,1,0:T(8,128)} %bitcast.13, f32[384,128]{1,0:T(8,128)} %bitcast.14, f32[2,48,2048]{2,1,0:T(8,128)} %azf_hbm.1, s32[16,128]{1,0:T(8,128)} %bitcast.15, s32[16,128]{1,0:T(8,128)} %bitcast.16, f32[8,16]{1,0:T(8,128)} %bitcast.17, ...), custom_call_target="tpu_custom_call" | custom-call | tf_op jit(solution)/shard_map/pallas_call | solution.py:783
  72.7 2.0 %shard_map.146 = f32[2,48,2048]{2,1,0:T(8,128)} custom-call(f32[2,16,48,128]{3,2,1,0:T(8,128)} %shard_map.145.f_hbm), custom_call_target="tpu_custom_call" | custom-call | tf_op jit(solution)/shard_map/pallas_call | solution.py:793

commit v9 on v7

--- a/solution.py
+++ b/solution.py
@@ -612,7 +612,7 @@
 
         lax.fori_loop(0, WINDOW // part, body, 0)
 
-    group = 4
+    group = 8
 
     def transform(from_core, add):
         def body(step, _):
@@ -763,8 +763,8 @@
         pltpu.VMEM((2, 16, BINS, LANES), F32),
         pltpu.VMEM((16, WINDOW, LANES), F32),
         pltpu.VMEM((16, 2, WINDOW, LANES), F32),
-        pltpu.VMEM((4, 2, WINDOW, LANES), F32),
-        pltpu.VMEM((4, 2, WINDOW, LANES), F32),
+        pltpu.VMEM((8, 2, WINDOW, LANES), F32),
+        pltpu.VMEM((8, 2, WINDOW, LANES), F32),
         pltpu.VMEM((2, 16, BINS, LANES), F32),
         DMA((2,)), DMA((4, 3)), DMA((4, 3)),
         DMA((len(BLOCKS),)), DMA((len(BLOCKS),)),

time: 74 us -> 73.2 us (0.989)
  no operation moved by 1% of the time
where the time goes in v9:
time: 73.2 us; the launch traced here: 72.9 us
  Pallas kernels  72.9 us (100%)
    pallas_call x1, Pallas kernels, shards(): pl.pallas_call(kernel, out_shape=jax.ShapeDtypeStruct((2, 16, BINS, LANES...  70.9 us
    pallas_call x1, Pallas kernels, shards(): pl.pallas_call(finish_kernel, out_shape=jax.ShapeDtypeStruct((2, BINS, PU...  2 us

profile of v9, /device:TPU:1, one launch (start us, length us, event | category | flops | bytes accessed | tf_op | source)
XLA Modules:
  0.0 72.9 jit_solution(4897932025298890661)
XLA Ops:
  0.0 70.9 %shard_map.145.f_hbm = f32[2,16,48,128]{3,2,1,0:T(8,128)} custom-call(f32[2,2,384,128]{3,2,1,0:T(8,128)} %bitcast.13, f32[384,128]{1,0:T(8,128)} %bitcast.14, f32[2,48,2048]{2,1,0:T(8,128)} %azf_hbm.1, s32[16,128]{1,0:T(8,128)} %bitcast.15, s32[16,128]{1,0:T(8,128)} %bitcast.16, f32[8,16]{1,0:T(8,128)} %bitcast.17, ...), custom_call_target="tpu_custom_call" | custom-call | tf_op jit(solution)/shard_map/pallas_call | solution.py:773
  70.9 2.0 %shard_map.146 = f32[2,48,2048]{2,1,0:T(8,128)} custom-call(f32[2,16,48,128]{3,2,1,0:T(8,128)} %shard_map.145.f_hbm), custom_call_target="tpu_custom_call" | custom-call | tf_op jit(solution)/shard_map/pallas_call | solution.py:783
